TPU v7x, 32 devices: a whole 2x2x4 slice. The times are simulated.
32 devices in a mesh: band: 8 (over y, x, core), grp: 4 (over z).
Axes of the slice: x: 2, y: 2, z: 4, core: 2. Of those that a mesh axis runs over, the one named last changes fastest.
Arguments:
- spectral: bfloat16 [640, 2, 4, 16, 640], P(('band', 'grp')), may hold values from -6 to 6
- legendre: bfloat16 [640, 640, 640], P(('band', 'grp')), may hold values from -4 to 4
- owner_table: int32 [640], replicated, may hold values from 0 to 639, as said below
Outputs:
- spectral_out: float32 [640, 2, 4, 16, 640], P(('band', 'grp'))
Inputs may be any that keep to these rules, and one draw needn't show every extreme that they name: `owner_table`: A permutation of the zonal wavenumbers. Slot s of the whole array belongs to device s // 20 along band+grp. For each q below 10, slots 2q and 2q + 1 of every device hold wavenumbers whose sum is (4q + 2) * 32 - 1.
All inputs are finite; a program needn't handle non-finite values.
Results may differ from a plain program's by a relative error of at most 0.0067.
Values may be sent and summed in bfloat16 or wider, within the bound.
No kernel may reach another device: no remote copies, remote signals or barrier semaphores. Data moves between devices by JAX's collectives and lax.ppermute only.
A program may use at most 192 MiB of HBM per device.

v0:
```python
import functools
import math

import jax
import jax.numpy as jnp
from jax import lax
from jax.experimental import pallas as pl
from jax.experimental.pallas import tpu as pltpu
from jax.sharding import PartitionSpec as P

LANES = 128
AXES = ("band", "grp")
VMEM_BYTES = 56 * 1024 * 1024
BRIEF = pl.CostEstimate(flops=10**6, bytes_accessed=10**4, transcendentals=0)


def synthesis_kernel(slots, levels, fields, least, scale, plane_ref, spec_ref, keep_ref, flip_ref, table_ref, *refs):
    out_refs, rows_ref = refs[:-1], refs[-1]
    tiles = rows_ref.shape[1]
    step = pl.program_id(0)
    block = spec_ref.shape[0]
    row_total = spec_ref.shape[1]
    stride = 2 * slots

    def run(group):
        start = least[group]
        for j in range(block):
            spec = spec_ref[j, :, start:]
            both = jnp.concatenate([spec * keep_ref[j, :, start:], spec * flip_ref[j, :, start:]], axis=0)
            halves = jnp.dot(both, table_ref[j, start:, :], preferred_element_type=jnp.float32) * scale
            first = 2 * (group * block + j)
            for hemi in range(2):
                for part in range(2):
                    for field in range(fields):
                        at = hemi * row_total + (part * fields + field) * levels
                        target = pl.ds(hemi * levels * stride + first + part, levels, stride=stride)
                        for tile in range(tiles):
                            lanes = slice(tile * LANES, (tile + 1) * LANES)
                            rows_ref[field, tile, target, :] = halves[at : at + levels, lanes]

    for group in range(slots // block):
        pl.when(step == group)(functools.partial(run, group))

    @pl.when(step == pl.num_programs(0) - 1)
    def _():
        for apart, out_ref in enumerate(out_refs):
            size = out_ref.shape[0]
            rows = pl.ds(pl.multiple_of(lax.rem(plane_ref[0] + apart, len(out_refs)) * size, size), size)
            for field in range(fields):
                for tile in range(tiles):
                    lanes = pl.ds((field * tiles + tile) * LANES, LANES)
                    out_ref[:, lanes] = rows_ref[field, tile, rows, :].astype(out_ref.dtype)


def synthesize(plane, planes, spec_rows, keep, flip, legendre, chunk, fields, levels, least):
    slots, row_total, degrees = spec_rows.shape
    block = slots // len(least)
    rows = 2 * levels * 2 * slots
    at, tiles = chunk
    shape = (rows // planes, fields * tiles * LANES)
    return pl.pallas_call(
        functools.partial(synthesis_kernel, slots, levels, fields, least, 1.0 / math.sqrt(degrees)),
        grid_spec=pltpu.PrefetchScalarGridSpec(
            num_scalar_prefetch=1,
            grid=(slots // block,),
            in_specs=[
                pl.BlockSpec((block, row_total, degrees), lambda i, _: (i, 0, 0)),
                pl.BlockSpec((block, 1, degrees), lambda i, _: (i, 0, 0)),
                pl.BlockSpec((block, 1, degrees), lambda i, _: (i, 0, 0)),
                pl.BlockSpec((block, degrees, tiles * LANES), lambda i, _: (i, 0, at // tiles)),
            ],
            out_specs=[pl.BlockSpec(shape, lambda i, _: (0, 0))] * planes,
            scratch_shapes=[pltpu.VMEM((fields, tiles, rows, LANES), jnp.float32)],
        ),
        out_shape=[jax.ShapeDtypeStruct(shape, jnp.bfloat16)] * planes,
        compiler_params=pltpu.CompilerParams(vmem_limit_bytes=VMEM_BYTES),
        cost_estimate=BRIEF,
        name="synthesis",
    )(plane, spec_rows, keep, flip, legendre)


def longitude_kernel(fields, grid_scale, zonal_scale, rows_ref, by_lon_ref, by_wave_ref, out_ref, sum_ref):
    step = pl.program_id(0)
    values = jnp.dot(by_lon_ref[...], rows_ref[...], preferred_element_type=jnp.float32) * grid_scale
    one = values.shape[1] // fields
    following = jnp.concatenate([values[:, one:], values[:, :one]], axis=1)
    product = (values * following).astype(jnp.bfloat16)
    share = jnp.dot(by_wave_ref[...], product, preferred_element_type=jnp.float32)

    @pl.when(step == 0)
    def _():
        sum_ref[...] = share

    @pl.when(step > 0)
    def _():
        sum_ref[...] += share

    @pl.when(step == pl.num_programs(0) - 1)
    def _():
        out_ref[...] = (sum_ref[...] * zonal_scale).astype(out_ref.dtype)


def longitudes(rows, by_lon, by_wave, fields):
    depth, width = rows.shape
    lon_count = by_lon.shape[0]
    lon_block = lon_count // 5
    return pl.pallas_call(
        functools.partial(longitude_kernel, fields, 1.0 / math.sqrt(depth // 2), 2.0 / math.sqrt(lon_count)),
        grid=(lon_count // lon_block,),
        in_specs=[
            pl.BlockSpec((depth, width), lambda i: (0, 0)),
            pl.BlockSpec((lon_block, depth), lambda i: (i, 0)),
            pl.BlockSpec((depth, lon_block), lambda i: (0, i)),
        ],
        out_specs=pl.BlockSpec((depth, width), lambda i: (0, 0)),
        out_shape=jax.ShapeDtypeStruct((depth, width), jnp.bfloat16),
        scratch_shapes=[pltpu.VMEM((depth, width), jnp.float32)],
        compiler_params=pltpu.CompilerParams(vmem_limit_bytes=VMEM_BYTES),
        cost_estimate=BRIEF,
        name="longitudes",
    )(rows, by_lon, by_wave)


def fold_kernel(slots, levels, fields, plane_ref, *refs):
    rows_refs, out_ref, rows_ref = refs[:-2], refs[-2], refs[-1]
    tiles = rows_ref.shape[1]
    stride = 2 * slots
    half = levels * stride
    for apart, arrived_ref in enumerate(rows_refs):
        size = arrived_ref.shape[0]
        rows = pl.ds(pl.multiple_of(lax.rem(plane_ref[0] + apart, len(rows_refs)) * size, size), size)
        for field in range(fields):
            for tile in range(tiles):
                lanes = pl.ds((field * tiles + tile) * LANES, LANES)
                rows_ref[field, tile, rows, :] = arrived_ref[:, lanes].astype(jnp.float32)
    for slot in range(slots):
        for part in range(2):
            for field in range(fields):
                for tile in range(tiles):
                    first = 2 * slot + part
                    north = rows_ref[field, tile, pl.ds(first, levels, stride=stride), :]
                    south = rows_ref[field, tile, pl.ds(half + first, levels, stride=stride), :]
                    lanes = pl.ds(tile * LANES, LANES)
                    at = (part * fields + field) * levels
                    out_ref[slot, at : at + levels, lanes] = (north + south).astype(out_ref.dtype)
                    at += 2 * fields * levels
                    out_ref[slot, at : at + levels, lanes] = (north - south).astype(out_ref.dtype)


def fold(plane, parts, slots, levels, fields):
    row_total = 2 * fields * levels
    rows = 2 * levels * 2 * slots
    tiles = parts[0].shape[1] // (fields * LANES)
    shape = (slots, 2 * row_total, tiles * LANES)
    size = rows * parts[0].shape[1]
    return pl.pallas_call(
        functools.partial(fold_kernel, slots, levels, fields),
        in_specs=[pl.BlockSpec(memory_space=pltpu.SMEM)] + [pl.BlockSpec(x.shape, lambda: (0, 0)) for x in parts],
        out_specs=pl.BlockSpec(shape, lambda: (0, 0, 0)),
        out_shape=jax.ShapeDtypeStruct(shape, jnp.bfloat16),
        scratch_shapes=[pltpu.VMEM((fields, tiles, rows, LANES), jnp.float32)],
        compiler_params=pltpu.CompilerParams(vmem_limit_bytes=VMEM_BYTES),
        cost_estimate=BRIEF,
        name="fold",
    )(plane, *parts)


def analysis_kernel(chunks, least, *refs):
    folded_refs = refs[:chunks]
    even_ref, odd_ref, table_ref, out_ref = refs[chunks:]
    row_total, degrees = out_ref.shape[1:]
    step = pl.program_id(0)

    def run(group):
        start = least[group]
        for j in range(out_ref.shape[0]):
            folded = jnp.concatenate([ref[j] for ref in folded_refs], axis=1)
            sums = lax.dot_general(
                folded, table_ref[j, start:, :], (((1,), (1,)), ((), ())), preferred_element_type=jnp.float32
            )
            kept = sums[:row_total] * even_ref[j, :, start:] + sums[row_total:] * odd_ref[j, :, start:]
            out_ref[j, :, start:] = kept
            if start:
                out_ref[j, :, :start] = jnp.zeros((row_total, start), out_ref.dtype)

    for group in range(len(least)):
        pl.when(step == group)(functools.partial(run, group))


def analyze(folded, even, odd, legendre, row_total, least):
    slots, degrees, lat_count = legendre.shape
    block = slots // len(least)
    mask_spec = pl.BlockSpec((block, 1, degrees), lambda i: (i, 0, 0))
    return pl.pallas_call(
        functools.partial(analysis_kernel, len(folded), least),
        grid=(len(least),),
        in_specs=[pl.BlockSpec((block,) + x.shape[1:], lambda i: (i, 0, 0)) for x in folded]
        + [mask_spec, mask_spec, pl.BlockSpec((block, degrees, lat_count), lambda i: (i, 0, 0))],
        out_specs=pl.BlockSpec((block, row_total, degrees), lambda i: (i, 0, 0)),
        out_shape=jax.ShapeDtypeStruct((slots, row_total, degrees), jnp.float32),
        compiler_params=pltpu.CompilerParams(vmem_limit_bytes=VMEM_BYTES),
        cost_estimate=pl.CostEstimate(
            flops=4 * slots * row_total * degrees * lat_count,
            bytes_accessed=2 * slots * (degrees * lat_count + 2 * row_total * (lat_count + degrees)),
            transcendentals=0,
        ),
        name="analysis",
    )(*folded, even, odd, legendre)


def trig_kernel(cos_base_ref, sin_base_ref, cos_turn_ref, sin_turn_ref, cos_base_t, sin_base_t, cos_turn_t, sin_turn_t, by_wave_ref, by_lon_ref):
    for j in range(cos_base_ref.shape[1]):
        lanes = pl.ds(j * LANES, LANES)
        cos_base, sin_base = cos_base_ref[:, j : j + 1], sin_base_ref[:, j : j + 1]
        angles = cos_base * cos_turn_ref[...] - sin_base * sin_turn_ref[...]
        by_wave_ref[:, lanes] = angles.astype(by_wave_ref.dtype)
        cos_base, sin_base = cos_base_t[j : j + 1, :], sin_base_t[j : j + 1, :]
        angles = cos_base * cos_turn_t[...] - sin_base * sin_turn_t[...]
        by_lon_ref[lanes, :] = angles.astype(by_lon_ref.dtype)


def trig_tables(owner_table, lon_count):
    waves = jnp.repeat(owner_table, 2).astype(jnp.float32)[:, None]
    quarter = jnp.tile(jnp.array([0, lon_count // 4], jnp.float32), owner_table.shape[0])[:, None]
    unit = 2.0 * math.pi / lon_count

    def angles(lon, turn):
        phase = waves * lon + turn
        return (phase - lon_count * jnp.floor(phase * (1.0 / lon_count))) * unit

    base = angles(jnp.arange(0, lon_count, LANES, dtype=jnp.float32)[None, :], quarter)
    turn = angles(jnp.arange(LANES, dtype=jnp.float32)[None, :], 0.0)
    depth = waves.shape[0]
    blocks = lon_count // LANES
    rows = 256
    small = pl.BlockSpec((rows, blocks), lambda i: (i, 0))
    wide = pl.BlockSpec((rows, LANES), lambda i: (i, 0))
    small_t = pl.BlockSpec((blocks, rows), lambda i: (0, i))
    wide_t = pl.BlockSpec((LANES, rows), lambda i: (0, i))
    parts = (jnp.cos(base), jnp.sin(base), jnp.cos(turn), jnp.sin(turn))
    return pl.pallas_call(
        trig_kernel,
        grid=(depth // rows,),
        in_specs=[small, small, wide, wide, small_t, small_t, wide_t, wide_t],
        out_specs=[
            pl.BlockSpec((rows, lon_count), lambda i: (i, 0)),
            pl.BlockSpec((lon_count, rows), lambda i: (0, i)),
        ],
        out_shape=[
            jax.ShapeDtypeStruct((depth, lon_count), jnp.bfloat16),
            jax.ShapeDtypeStruct((lon_count, depth), jnp.bfloat16),
        ],
        compiler_params=pltpu.CompilerParams(vmem_limit_bytes=VMEM_BYTES),
        cost_estimate=BRIEF,
        name="trig",
    )(*parts, *[x.T for x in parts])


def across_planes(parts, way):
    planes = len(parts)
    return [parts[0]] + [
        lax.ppermute(parts[x], "grp", [(p, (p + way * x) % planes) for p in range(planes)]) for x in range(1, planes)
    ]


def within_plane(rows):
    bands = lax.axis_size("band")
    cut = rows.reshape(bands, -1, rows.shape[-1])
    return lax.all_to_all(cut, "band", split_axis=0, concat_axis=0, tiled=True)


def after(value, *others):
    return lax.optimization_barrier((value, others))[0]


def by_hemisphere_and_level(spectral, legendre, owner_table):
    slots, _, fields, levels, degrees = spectral.shape
    half_lat = legendre.shape[2]
    lon_count = 4 * half_lat
    row_total = 2 * fields * levels
    tiles = half_lat // LANES
    wavenumber = lax.dynamic_slice_in_dim(owner_table, lax.axis_index(AXES) * slots, slots)
    distance = jnp.arange(degrees, dtype=jnp.int32)[None, :] - wavenumber[:, None]
    kept = distance >= 0
    is_odd = distance % 2 != 0
    keep = kept.astype(jnp.bfloat16)[:, None, :]
    flip = jnp.where(is_odd, -keep[:, 0], keep[:, 0])[:, None, :]
    scale = 1.0 / math.sqrt(2 * half_lat)
    even = jnp.where(kept & ~is_odd, scale, 0.0).astype(jnp.float32)[:, None, :]
    odd = jnp.where(kept & is_odd, scale, 0.0).astype(jnp.float32)[:, None, :]
    spec_rows = spectral.reshape(slots, row_total, degrees)
    planes, bands = lax.axis_size("grp"), lax.axis_size("band")
    plane = lax.axis_index("grp")
    sources = (plane + planes - jnp.arange(planes, dtype=jnp.int32)) % planes
    owners = jnp.take(owner_table.reshape(bands, planes, slots), sources, axis=1).reshape(-1)
    plane = plane.reshape(1)
    least = tuple(4 * g * bands * planes for g in range(slots // 4))

    def send(spec, tile):
        return synthesize(plane, planes, spec, keep, flip, legendre, (tile, 1), fields, levels, least)

    def stack(parts):
        width = parts[0].shape[-1]
        return jnp.stack([x.reshape(bands, -1, width) for x in parts], axis=1)

    def give_back(cut, *others):
        width = cut.shape[-1]
        cut = cut.reshape(bands, planes, -1, width)
        parts = [cut[:, x].reshape(-1, width) for x in range(planes)]
        return across_planes(after(parts, *others), -1)

    sent, moved, arrived, zonal, cuts, folded = [], [], [], [], [], []
    for t in range(tiles + 2):
        if t < tiles:
            spec = spec_rows
            if t == 1:
                by_wave, by_lon = trig_tables(owners, lon_count)
                spec = after(spec_rows, by_wave)
            elif t >= 2:
                spec = after(spec_rows, *moved[t - 2])
            sent.append(send(spec, t))
            moved.append(across_planes(sent[t], 1))
        if t >= 1 and t - 1 < tiles:
            ready = after(moved[t - 1], *sent[t]) if t < tiles else moved[t - 1]
            if t >= 3:
                ready = after(ready, cuts[t - 3])
            arrived.append(within_plane(stack(ready)))
        if t >= 2:
            rows = arrived[t - 2]
            values = longitudes(rows.reshape(-1, rows.shape[-1]), by_lon, by_wave, fields)
            if t - 1 < tiles:
                values = after(values, arrived[t - 1])
            cuts.append(within_plane(values))
    for t in range(tiles):
        parts = give_back(cuts[t], *([folded[t - 2]] if t >= 2 else []))
        folded.append(fold(plane, parts, slots, levels, fields))
    out = analyze(folded, even, odd, legendre, row_total, least)
    return out.reshape(slots, 2, fields, levels, degrees)


def make_trig(wavenumber, lon_count):
    lon_index = jnp.arange(lon_count, dtype=jnp.int32)
    phases = wavenumber[:, None] * lon_index[None, :] % lon_count
    angles = phases.astype(jnp.float32) * (2.0 * math.pi / lon_count)
    return jnp.stack([jnp.cos(angles), -jnp.sin(angles)], axis=1).astype(jnp.bfloat16)


def by_level_and_latitude(spectral, legendre, owner_table):
    slot_count, _, fields, levels, degrees = spectral.shape
    half_lat = legendre.shape[2]
    lat_count = 2 * half_lat
    lon_count = 2 * lat_count
    wave_count = owner_table.shape[0]
    band_count = lax.axis_size("band")
    group_count = lax.axis_size("grp")
    device_count = band_count * group_count
    level_block = levels // band_count
    lat_block = lat_count // group_count
    row_total = 2 * fields * levels
    row_width = fields * level_block * lat_block
    slot_start = lax.axis_index(("band", "grp")) * slot_count
    wavenumber = lax.dynamic_slice_in_dim(owner_table, slot_start, slot_count)
    degree_index = jnp.arange(degrees, dtype=jnp.int32)
    keep_mask = (degree_index[None, :] >= wavenumber[:, None]).astype(jnp.bfloat16)
    odd_part = (degree_index[None, :] - wavenumber[:, None]) % 2
    flip_sign = (1 - 2 * odd_part).astype(jnp.bfloat16)
    spec_rows = spectral.reshape(slot_count, row_total, degrees) * keep_mask[:, None, :]
    both_rows = jnp.concatenate([spec_rows, spec_rows * flip_sign[:, None, :]], axis=1)
    halves = jnp.einsum("srn,snt->srt", both_rows, legendre, preferred_element_type=jnp.float32)
    northern = halves[:, :row_total]
    mirrored = halves[:, row_total:]
    fourier = jnp.concatenate([northern, jnp.flip(mirrored, axis=2)], axis=2)
    fourier = fourier.reshape(
        slot_count, 2, fields, band_count, level_block, group_count, lat_block
    )
    fourier = jnp.transpose(fourier, (0, 1, 2, 3, 5, 4, 6))
    fourier_low = (fourier * (1.0 / math.sqrt(degrees))).astype(jnp.bfloat16)
    packed = fourier_low.reshape(1, slot_count, 2, fields, device_count, level_block, lat_block)
    arrived = lax.all_to_all(packed, ("band", "grp"), split_axis=4, concat_axis=0, tiled=True)
    arrived = arrived.reshape(-1, 2, row_width)
    trig_rows = make_trig(owner_table, lon_count)
    grid_values = jnp.einsum("scw,scl->wl", arrived, trig_rows, preferred_element_type=jnp.float32)
    grid_values = (grid_values * (1.0 / math.sqrt(wave_count))).reshape(
        fields, level_block * lat_block, lon_count
    )
    product = (grid_values * jnp.roll(grid_values, -1, axis=0)).astype(jnp.bfloat16)
    zonal_coeffs = jnp.einsum(
        "wl,scl->scw",
        product.reshape(row_width, lon_count),
        trig_rows,
        preferred_element_type=jnp.float32,
    )
    zonal_coeffs = (zonal_coeffs * (2.0 / math.sqrt(lon_count))).astype(jnp.bfloat16)
    sendback = zonal_coeffs.reshape(device_count, slot_count, 2, fields, 1, level_block, lat_block)
    returned = lax.all_to_all(sendback, ("band", "grp"), split_axis=0, concat_axis=4, tiled=True)
    returned = returned.reshape(
        slot_count, 2, fields, band_count, group_count, level_block, lat_block
    )
    returned = jnp.transpose(returned, (0, 1, 2, 3, 5, 4, 6)).reshape(slot_count, row_total, lat_count)
    northern_part = returned[:, :, :half_lat].astype(jnp.float32)
    mirror_part = jnp.flip(returned[:, :, half_lat:], axis=2).astype(jnp.float32)
    plus_part = (northern_part + mirror_part).astype(jnp.bfloat16)
    minus_part = (northern_part - mirror_part).astype(jnp.bfloat16)
    stacked = jnp.concatenate([plus_part, minus_part], axis=1)
    projected = jnp.einsum("srt,snt->srn", stacked, legendre, preferred_element_type=jnp.float32)
    even_rows = flip_sign[:, None, :] > 0
    chosen = jnp.where(even_rows, projected[:, :row_total], projected[:, row_total:])
    chosen = chosen * keep_mask.astype(jnp.float32)[:, None, :] * (1.0 / math.sqrt(lat_count))
    return chosen.reshape(slot_count, 2, fields, levels, degrees)


def on_device(spectral, legendre, owner_table):
    slots, _, _, levels, _ = spectral.shape
    planes = lax.axis_size("grp")
    whole_hemispheres = lax.axis_size("band") * planes == 2 * levels and planes & (planes - 1) == 0
    if whole_hemispheres and legendre.shape[2] % LANES == 0 and slots % 4 == 0 and levels % 8 == 0:
        return by_hemisphere_and_level(spectral, legendre, owner_table)
    return by_level_and_latitude(spectral, legendre, owner_table)


def solution(mesh):
    placed = (P(("band", "grp"), None, None, None, None), P(("band", "grp"), None, None), P())
    return jax.shard_map(
        on_device,
        mesh=mesh,
        in_specs=placed,
        out_specs=P(("band", "grp"), None, None, None, None),
        check_vma=False,
    )
```

profile of v0, /device:TPU:0, one launch (start us, length us, event | category | flops | bytes accessed | tf_op | source)
XLA Modules:
  0.0 487.1 jit_solution(13707911854827317080)
XLA Ops:
  2.4 6.6 %synthesis.5 = (bf16[320,512]{1,0:T(8,128)(2,1)}, bf16[320,512]{1,0:T(8,128)(2,1)}, bf16[320,512]{1,0:T(8,128)(2,1)}, bf16[320,512]{1,0:T(8,128)(2,1)}) custom-call(s32[1]{0:T(128)} %bitcast.plane_ref, bf16[20,128,640]{2,1,0:T(8,128)(2,1)} %bitcast.67, bf16[20,1,640]{2,1,0:T(2,128)(2,1)} %fusion.11.keep_ref, bf16[20,1,640]{2,1,0:T(2,128)(2,1)} %negate_select_fusion.flip_ref, ...), custom_call_target="tpu_custom_call" | custom-call | flops 1000000 | bytes 10000 | tf_op jit(solution)/shard_map/synthesis/pallas_call | solution.py:61
  30.2 11.8 %trig.1 = (bf16[1280,2560]{1,0:T(8,128)(2,1)}, bf16[2560,1280]{1,0:T(8,128)(2,1)}) custom-call(f32[1280,20]{1,0:T(8,128)} %get-tuple-element.184.cos_base_ref, f32[1280,20]{1,0:T(8,128)} %get-tuple-element.183.sin_base_ref, f32[1280,128]{1,0:T(8,128)} %get-tuple-element.188.cos_turn_ref, f32[1280,128]{1,0:T(8,128)} %get-tuple-element.187.sin_turn_ref, ...), custom_call_target="tpu_custom_call" | custom-call | flops 1000000 | bytes 10000 | tf_op jit(solution)/shard_map/trig/pallas_call | solution.py:241
  66.4 13.6 %collective-permute-done.4 = bf16[320,512]{1,0:T(8,128)(2,1)S(1)} collective-permute-done((bf16[320,512]{1,0:T(8,128)(2,1)S(1)}, bf16[320,512]{1,0:T(8,128)(2,1)S(1)}, u32[]{:S(2)}, u32[]{:S(2)}) %collective-permute-start.4) | collective-permute-done | bytes 327712 | tf_op jit(solution)/shard_map/ppermute | solution.py:262
  86.4 12.6 %longitudes.5 = bf16[1280,512]{1,0:T(8,128)(2,1)} custom-call(bf16[1280,512]{1,0:T(8,128)(2,1)} %bitcast.79, bf16[2560,1280]{1,0:T(8,128)(2,1)} %get-tuple-element.97.by_lon_ref, bf16[1280,2560]{1,0:T(8,128)(2,1)} %get-tuple-element.87.by_wave_ref), custom_call_target="tpu_custom_call" | custom-call | flops 1000000 | bytes 10000 | tf_op jit(solution)/shard_map/longitudes/pallas_call | solution.py:107
  109.3 7.0 %collective-permute-start.9 = (bf16[320,512]{1,0:T(8,128)(2,1)}, bf16[320,512]{1,0:T(8,128)(2,1)S(1)}, u32[]{:S(2)}, u32[]{:S(2)}) collective-permute-start(bf16[320,512]{1,0:T(8,128)(2,1)} %get-tuple-element.100), channel_id=1, source_target_pairs={{0,1},{1,2},{2,3},{3,0},{4,5},{5,6},{6,7},{7,4},{8,9},{9,10},{10,1... | collective-permute-start | bytes 983048 | tf_op jit(solution)/shard_map/ppermute | solution.py:262
  118.8 6.6 %synthesis.8 = (bf16[320,512]{1,0:T(8,128)(2,1)}, bf16[320,512]{1,0:T(8,128)(2,1)}, bf16[320,512]{1,0:T(8,128)(2,1)}, bf16[320,512]{1,0:T(8,128)(2,1)}) custom-call(s32[1]{0:T(128)} %bitcast.plane_ref, bf16[20,128,640]{2,1,0:T(8,128)(2,1)} %bitcast.70, bf16[20,1,640]{2,1,0:T(2,128)(2,1)} %fusion.11.keep_ref, bf16[20,1,640]{2,1,0:T(2,128)(2,1)} %negate_select_fusion.flip_ref, ...), custom_call_target="tpu_custom_call" | custom-call | flops 1000000 | bytes 10000 | tf_op jit(solution)/shard_map/synthesis/pallas_call | solution.py:61
  125.4 12.9 %collective-permute-done.10 = bf16[320,512]{1,0:T(8,128)(2,1)S(1)} collective-permute-done((bf16[320,512]{1,0:T(8,128)(2,1)S(1)}, bf16[320,512]{1,0:T(8,128)(2,1)S(1)}, u32[]{:S(2)}, u32[]{:S(2)}) %collective-permute-start.10) | collective-permute-done | bytes 327712 | tf_op jit(solution)/shard_map/ppermute | solution.py:262
  143.6 12.6 %longitudes.6 = bf16[1280,512]{1,0:T(8,128)(2,1)} custom-call(bf16[1280,512]{1,0:T(8,128)(2,1)} %bitcast.78, bf16[2560,1280]{1,0:T(8,128)(2,1)} %get-tuple-element.97.by_lon_ref, bf16[1280,2560]{1,0:T(8,128)(2,1)} %get-tuple-element.87.by_wave_ref), custom_call_target="tpu_custom_call" | custom-call | flops 1000000 | bytes 10000 | tf_op jit(solution)/shard_map/longitudes/pallas_call | solution.py:107
  166.5 7.5 %collective-permute-start.15 = (bf16[320,512]{1,0:T(8,128)(2,1)}, bf16[320,512]{1,0:T(8,128)(2,1)S(1)}, u32[]{:S(2)}, u32[]{:S(2)}) collective-permute-start(bf16[320,512]{1,0:T(8,128)(2,1)} %get-tuple-element.114), channel_id=1, source_target_pairs={{0,1},{1,2},{2,3},{3,0},{4,5},{5,6},{6,7},{7,4},{8,9},{9,10},{10,1... | collective-permute-start | bytes 983048 | tf_op jit(solution)/shard_map/ppermute | solution.py:262
  185.3 13.7 %collective-permute-done.16 = bf16[320,512]{1,0:T(8,128)(2,1)S(1)} collective-permute-done((bf16[320,512]{1,0:T(8,128)(2,1)}, bf16[320,512]{1,0:T(8,128)(2,1)S(1)}, u32[]{:S(2)}, u32[]{:S(2)}) %collective-permute-start.16) | collective-permute-done | bytes 327712 | tf_op jit(solution)/shard_map/ppermute | solution.py:262
  206.8 12.6 %longitudes.7 = bf16[1280,512]{1,0:T(8,128)(2,1)} custom-call(bf16[1280,512]{1,0:T(8,128)(2,1)} %bitcast.77, bf16[2560,1280]{1,0:T(8,128)(2,1)} %get-tuple-element.97.by_lon_ref, bf16[1280,2560]{1,0:T(8,128)(2,1)} %get-tuple-element.87.by_wave_ref), custom_call_target="tpu_custom_call" | custom-call | flops 1000000 | bytes 10000 | tf_op jit(solution)/shard_map/longitudes/pallas_call | solution.py:107
  229.5 7.5 %collective-permute-start.21 = (bf16[320,512]{1,0:T(8,128)(2,1)}, bf16[320,512]{1,0:T(8,128)(2,1)S(1)}, u32[]{:S(2)}, u32[]{:S(2)}) collective-permute-start(bf16[320,512]{1,0:T(8,128)(2,1)} %get-tuple-element.132), channel_id=1, source_target_pairs={{0,1},{1,2},{2,3},{3,0},{4,5},{5,6},{6,7},{7,4},{8,9},{9,10},{10,1... | collective-permute-start | bytes 983048 | tf_op jit(solution)/shard_map/ppermute | solution.py:262
  245.3 13.8 %collective-permute-done.22 = bf16[320,512]{1,0:T(8,128)(2,1)} collective-permute-done((bf16[320,512]{1,0:T(8,128)(2,1)}, bf16[320,512]{1,0:T(8,128)(2,1)}, u32[]{:S(2)}, u32[]{:S(2)}) %collective-permute-start.22) | collective-permute-done | bytes 327712 | tf_op jit(solution)/shard_map/ppermute | solution.py:262
  265.9 12.6 %longitudes.8 = bf16[1280,512]{1,0:T(8,128)(2,1)} custom-call(bf16[1280,512]{1,0:T(8,128)(2,1)} %bitcast.45.rows_ref, bf16[2560,1280]{1,0:T(8,128)(2,1)} %get-tuple-element.97.by_lon_ref, bf16[1280,2560]{1,0:T(8,128)(2,1)} %get-tuple-element.87.by_wave_ref), custom_call_target="tpu_custom_call" | custom-call | flops 1000000 | bytes 10000 | tf_op jit(solution)/shard_map/longitudes/pallas_call | solution.py:107
  288.4 12.6 %longitudes.9 = bf16[1280,512]{1,0:T(8,128)(2,1)} custom-call(bf16[1280,512]{1,0:T(8,128)(2,1)} %bitcast.57.rows_ref, bf16[2560,1280]{1,0:T(8,128)(2,1)} %get-tuple-element.97.by_lon_ref, bf16[1280,2560]{1,0:T(8,128)(2,1)} %get-tuple-element.87.by_wave_ref), custom_call_target="tpu_custom_call" | custom-call | flops 1000000 | bytes 10000 | tf_op jit(solution)/shard_map/longitudes/pallas_call | solution.py:107
  311.7 9.8 %collective-permute-start.6 = (bf16[320,512]{1,0:T(8,128)(2,1)S(1)}, bf16[320,512]{1,0:T(8,128)(2,1)S(1)}, u32[]{:S(2)}, u32[]{:S(2)}) collective-permute-start(bf16[320,512]{1,0:T(8,128)(2,1)S(1)} %bitcast.114), channel_id=1, source_target_pairs={{0,3},{1,0},{2,1},{3,2},{4,7},{5,4},{6,5},{7,6},{8,11},{9,8},{10,9... | collective-permute-start | bytes 983048 | tf_op jit(solution)/shard_map/ppermute | solution.py:262
  329.8 20.5 %collective-permute-done.7.refs_2_ = bf16[320,512]{1,0:T(8,128)(2,1)S(1)} collective-permute-done((bf16[320,512]{1,0:T(8,128)(2,1)S(1)}, bf16[320,512]{1,0:T(8,128)(2,1)S(1)}, u32[]{:S(2)}, u32[]{:S(2)}) %collective-permute-start.7) | collective-permute-done | bytes 327712 | tf_op jit(solution)/shard_map/ppermute | solution.py:262
  356.8 16.4 %collective-permute-start.19 = (bf16[320,512]{1,0:T(8,128)(2,1)S(1)}, bf16[320,512]{1,0:T(8,128)(2,1)S(1)}, u32[]{:S(2)}, u32[]{:S(2)}) collective-permute-start(bf16[320,512]{1,0:T(8,128)(2,1)S(1)} %bitcast.104), channel_id=1, source_target_pairs={{0,2},{1,3},{2,0},{3,1},{4,6},{5,7},{6,4},{7,5},{8,10},{9,11},{10,... | collective-permute-start | bytes 983048 | tf_op jit(solution)/shard_map/ppermute | solution.py:262
  384.8 10.8 %collective-permute-start.24 = (bf16[320,512]{1,0:T(8,128)(2,1)S(1)}, bf16[320,512]{1,0:T(8,128)(2,1)S(1)}, u32[]{:S(2)}, u32[]{:S(2)}) collective-permute-start(bf16[320,512]{1,0:T(8,128)(2,1)S(1)} %bitcast.101), channel_id=1, source_target_pairs={{0,3},{1,0},{2,1},{3,2},{4,7},{5,4},{6,5},{7,6},{8,11},{9,8},{10,9... | collective-permute-start | bytes 983048 | tf_op jit(solution)/shard_map/ppermute | solution.py:262
  395.6 10.9 %collective-permute-done.19.refs_2_ = bf16[320,512]{1,0:T(8,128)(2,1)S(1)} collective-permute-done((bf16[320,512]{1,0:T(8,128)(2,1)S(1)}, bf16[320,512]{1,0:T(8,128)(2,1)S(1)}, u32[]{:S(2)}, u32[]{:S(2)}) %collective-permute-start.19) | collective-permute-done | bytes 327712 | tf_op jit(solution)/shard_map/ppermute | solution.py:262
  410.9 8.6 %collective-permute-start.25 = (bf16[320,512]{1,0:T(8,128)(2,1)S(1)}, bf16[320,512]{1,0:T(8,128)(2,1)S(1)}, u32[]{:S(2)}, u32[]{:S(2)}) collective-permute-start(bf16[320,512]{1,0:T(8,128)(2,1)S(1)} %bitcast.97), channel_id=1, source_target_pairs={{0,2},{1,3},{2,0},{3,1},{4,6},{5,7},{6,4},{7,5},{8,10},{9,11},{10,... | collective-permute-start | bytes 983048 | tf_op jit(solution)/shard_map/ppermute | solution.py:262
  427.3 15.4 %collective-permute-done.25.refs_2_ = bf16[320,512]{1,0:T(8,128)(2,1)S(1)} collective-permute-done((bf16[320,512]{1,0:T(8,128)(2,1)S(1)}, bf16[320,512]{1,0:T(8,128)(2,1)S(1)}, u32[]{:S(2)}, u32[]{:S(2)}) %collective-permute-start.25) | collective-permute-done | bytes 327712 | tf_op jit(solution)/shard_map/ppermute | solution.py:262
  447.1 22.0 %collective-permute-done.28.refs_2_ = bf16[320,512]{1,0:T(8,128)(2,1)S(1)} collective-permute-done((bf16[320,512]{1,0:T(8,128)(2,1)S(1)}, bf16[320,512]{1,0:T(8,128)(2,1)S(1)}, u32[]{:S(2)}, u32[]{:S(2)}) %collective-permute-start.28) | collective-permute-done | bytes 327712 | tf_op jit(solution)/shard_map/ppermute | solution.py:262
  473.5 13.2 %analysis.1 = f32[20,128,640]{2,1,0:T(8,128)} custom-call(bf16[20,256,128]{2,1,0:T(8,128)(2,1)} %fold.5.refs_0_, bf16[20,256,128]{2,1,0:T(8,128)(2,1)} %fold.6.refs_1_, bf16[20,256,128]{2,1,0:T(8,128)(2,1)} %fold.7.refs_2_, bf16[20,256,128]{2,1,0:T(8,128)(2,1)} %fold.8.refs_3_, bf16[20,256,128]{2,1,0:T(8,128)(2,1)} %fold.9.refs_4_, ...), custom_call_target="tpu_custom_call" | custom-call | flops 4194304000 | bytes 29491200 | tf_op jit(solution)/shard_map/analysis/pallas_call | solution.py:194
  (174 shorter events, 194.7 us)
Async XLA Ops:
  9.0 39.5 %collective-permute-start = (bf16[320,512]{1,0:T(8,128)(2,1)}, bf16[320,512]{1,0:T(8,128)(2,1)S(1)}, u32[]{:S(2)}, u32[]{:S(2)}) collective-permute-start(bf16[320,512]{1,0:T(8,128)(2,1)} %get-tuple-element.84), channel_id=1, source_target_pairs={{0,1},{1,2},{2,3},{3,0},{4,5},{5,6},{6,7},{7,4},{8,9},{9,10},{10,1... | collective-permute-start | bytes 983048 | tf_op jit(solution)/shard_map/ppermute | solution.py:262
  12.0 36.5 %collective-permute-start.1 = (bf16[320,512]{1,0:T(8,128)(2,1)}, bf16[320,512]{1,0:T(8,128)(2,1)S(1)}, u32[]{:S(2)}, u32[]{:S(2)}) collective-permute-start(bf16[320,512]{1,0:T(8,128)(2,1)} %get-tuple-element.85), channel_id=1, source_target_pairs={{0,2},{1,3},{2,0},{3,1},{4,6},{5,7},{6,4},{7,5},{8,10},{9,11},{10,... | collective-permute-start | bytes 983048 | tf_op jit(solution)/shard_map/ppermute | solution.py:262
  14.6 33.9 %collective-permute-start.2 = (bf16[320,512]{1,0:T(8,128)(2,1)}, bf16[320,512]{1,0:T(8,128)(2,1)S(1)}, u32[]{:S(2)}, u32[]{:S(2)}) collective-permute-start(bf16[320,512]{1,0:T(8,128)(2,1)} %get-tuple-element.86), channel_id=1, source_target_pairs={{0,3},{1,0},{2,1},{3,2},{4,7},{5,4},{6,5},{7,6},{8,11},{9,8},{10,9... | collective-permute-start | bytes 983048 | tf_op jit(solution)/shard_map/ppermute | solution.py:262
  50.0 31.3 %all-to-all-start = ((bf16[8,160,512]{2,1,0:T(8,128)(2,1)}), bf16[8,160,512]{2,1,0:T(8,128)(2,1)S(1)}, u32[]{:S(2)}, u32[]{:S(2)}) async-start(bf16[8,160,512]{2,1,0:T(8,128)(2,1)} %bitcast.8), calls=%async_computation | async-start | bytes 2621440 | tf_op jit(solution)/shard_map/all_to_all | solution.py:269
  54.6 25.4 %collective-permute-start.4 = (bf16[320,512]{1,0:T(8,128)(2,1)S(1)}, bf16[320,512]{1,0:T(8,128)(2,1)S(1)}, u32[]{:S(2)}, u32[]{:S(2)}) collective-permute-start(bf16[320,512]{1,0:T(8,128)(2,1)S(1)} %copy-done.30), channel_id=1, source_target_pairs={{0,2},{1,3},{2,0},{3,1},{4,6},{5,7},{6,4},{7,5},{8,10},{9,11},{10,... | collective-permute-start | bytes 983048 | tf_op jit(solution)/shard_map/ppermute | solution.py:262
  54.9 25.0 %collective-permute-start.5 = (bf16[320,512]{1,0:T(8,128)(2,1)S(1)}, bf16[320,512]{1,0:T(8,128)(2,1)S(1)}, u32[]{:S(2)}, u32[]{:S(2)}) collective-permute-start(bf16[320,512]{1,0:T(8,128)(2,1)S(1)} %copy-done.29), channel_id=1, source_target_pairs={{0,3},{1,0},{2,1},{3,2},{4,7},{5,4},{6,5},{7,6},{8,11},{9,8},{10,9... | collective-permute-start | bytes 983048 | tf_op jit(solution)/shard_map/ppermute | solution.py:262
  105.7 32.6 %all-to-all-start.2 = ((bf16[8,160,512]{2,1,0:T(8,128)(2,1)}), bf16[8,160,512]{2,1,0:T(8,128)(2,1)S(1)}, u32[]{:S(2)}, u32[]{:S(2)}) async-start(bf16[8,160,512]{2,1,0:T(8,128)(2,1)} %bitcast.81), calls=%async_computation.2 | async-start | bytes 2621440 | tf_op jit(solution)/shard_map/all_to_all | solution.py:269
  162.9 36.9 %all-to-all-start.4 = ((bf16[8,160,512]{2,1,0:T(8,128)(2,1)}), bf16[8,160,512]{2,1,0:T(8,128)(2,1)S(1)}, u32[]{:S(2)}, u32[]{:S(2)}) async-start(bf16[8,160,512]{2,1,0:T(8,128)(2,1)} %bitcast.80), calls=%async_computation.4 | async-start | bytes 2621440 | tf_op jit(solution)/shard_map/all_to_all | solution.py:269
  174.1 24.9 %collective-permute-start.16 = (bf16[320,512]{1,0:T(8,128)(2,1)}, bf16[320,512]{1,0:T(8,128)(2,1)S(1)}, u32[]{:S(2)}, u32[]{:S(2)}) collective-permute-start(bf16[320,512]{1,0:T(8,128)(2,1)} %get-tuple-element.115), channel_id=1, source_target_pairs={{0,2},{1,3},{2,0},{3,1},{4,6},{5,7},{6,4},{7,5},{8,10},{9,11},{10,... | collective-permute-start | bytes 983048 | tf_op jit(solution)/shard_map/ppermute | solution.py:262
  225.1 34.1 %all-to-all-start.6 = ((bf16[8,160,512]{2,1,0:T(8,128)(2,1)}), bf16[8,160,512]{2,1,0:T(8,128)(2,1)}, u32[]{:S(2)}, u32[]{:S(2)}) async-start(bf16[8,160,512]{2,1,0:T(8,128)(2,1)} %bitcast.82), calls=%async_computation.6 | async-start | bytes 2621440 | tf_op jit(solution)/shard_map/all_to_all | solution.py:269
  306.6 112.9 %all-to-all-start.9 = ((bf16[8,160,512]{2,1,0:T(8,128)(2,1)}), bf16[8,160,512]{2,1,0:T(8,128)(2,1)}, u32[]{:S(2)}, u32[]{:S(2)}) async-start(bf16[8,160,512]{2,1,0:T(8,128)(2,1)} %bitcast.76), calls=%async_computation.9 | async-start | bytes 2621440 | tf_op jit(solution)/shard_map/all_to_all | solution.py:269
  321.5 28.8 %collective-permute-start.7 = (bf16[320,512]{1,0:T(8,128)(2,1)S(1)}, bf16[320,512]{1,0:T(8,128)(2,1)S(1)}, u32[]{:S(2)}, u32[]{:S(2)}) collective-permute-start(bf16[320,512]{1,0:T(8,128)(2,1)S(1)} %bitcast.109), channel_id=1, source_target_pairs={{0,2},{1,3},{2,0},{3,1},{4,6},{5,7},{6,4},{7,5},{8,10},{9,11},{10,... | collective-permute-start | bytes 983048 | tf_op jit(solution)/shard_map/ppermute | solution.py:262
  321.5 28.8 %collective-permute-start.8 = (bf16[320,512]{1,0:T(8,128)(2,1)S(1)}, bf16[320,512]{1,0:T(8,128)(2,1)S(1)}, u32[]{:S(2)}, u32[]{:S(2)}) collective-permute-start(bf16[320,512]{1,0:T(8,128)(2,1)S(1)} %bitcast.107), channel_id=1, source_target_pairs={{0,1},{1,2},{2,3},{3,0},{4,5},{5,6},{6,7},{7,4},{8,9},{9,10},{10,1... | collective-permute-start | bytes 983048 | tf_op jit(solution)/shard_map/ppermute | solution.py:262
  322.9 50.3 %collective-permute-start.12 = (bf16[320,512]{1,0:T(8,128)(2,1)S(1)}, bf16[320,512]{1,0:T(8,128)(2,1)S(1)}, u32[]{:S(2)}, u32[]{:S(2)}) collective-permute-start(bf16[320,512]{1,0:T(8,128)(2,1)S(1)} %bitcast.103), channel_id=1, source_target_pairs={{0,3},{1,0},{2,1},{3,2},{4,7},{5,4},{6,5},{7,6},{8,11},{9,8},{10,9... | collective-permute-start | bytes 983048 | tf_op jit(solution)/shard_map/ppermute | solution.py:262
  326.2 52.2 %collective-permute-start.13 = (bf16[320,512]{1,0:T(8,128)(2,1)S(1)}, bf16[320,512]{1,0:T(8,128)(2,1)S(1)}, u32[]{:S(2)}, u32[]{:S(2)}) collective-permute-start(bf16[320,512]{1,0:T(8,128)(2,1)S(1)} %bitcast.100), channel_id=1, source_target_pairs={{0,2},{1,3},{2,0},{3,1},{4,6},{5,7},{6,4},{7,5},{8,10},{9,11},{10,... | collective-permute-start | bytes 983048 | tf_op jit(solution)/shard_map/ppermute | solution.py:262
  329.6 48.8 %collective-permute-start.14 = (bf16[320,512]{1,0:T(8,128)(2,1)S(1)}, bf16[320,512]{1,0:T(8,128)(2,1)S(1)}, u32[]{:S(2)}, u32[]{:S(2)}) collective-permute-start(bf16[320,512]{1,0:T(8,128)(2,1)S(1)} %bitcast.98), channel_id=1, source_target_pairs={{0,1},{1,2},{2,3},{3,0},{4,5},{5,6},{6,7},{7,4},{8,9},{9,10},{10,1... | collective-permute-start | bytes 983048 | tf_op jit(solution)/shard_map/ppermute | solution.py:262
  356.8 38.9 %collective-permute-start.18 = (bf16[320,512]{1,0:T(8,128)(2,1)S(1)}, bf16[320,512]{1,0:T(8,128)(2,1)S(1)}, u32[]{:S(2)}, u32[]{:S(2)}) collective-permute-start(bf16[320,512]{1,0:T(8,128)(2,1)S(1)} %bitcast.105), channel_id=1, source_target_pairs={{0,3},{1,0},{2,1},{3,2},{4,7},{5,4},{6,5},{7,6},{8,11},{9,8},{10,9... | collective-permute-start | bytes 983048 | tf_op jit(solution)/shard_map/ppermute | solution.py:262
  356.8 49.7 %collective-permute-start.19 = (bf16[320,512]{1,0:T(8,128)(2,1)S(1)}, bf16[320,512]{1,0:T(8,128)(2,1)S(1)}, u32[]{:S(2)}, u32[]{:S(2)}) collective-permute-start(bf16[320,512]{1,0:T(8,128)(2,1)S(1)} %bitcast.104), channel_id=1, source_target_pairs={{0,2},{1,3},{2,0},{3,1},{4,6},{5,7},{6,4},{7,5},{8,10},{9,11},{10,... | collective-permute-start | bytes 983048 | tf_op jit(solution)/shard_map/ppermute | solution.py:262
  373.2 33.4 %collective-permute-start.20 = (bf16[320,512]{1,0:T(8,128)(2,1)S(1)}, bf16[320,512]{1,0:T(8,128)(2,1)S(1)}, u32[]{:S(2)}, u32[]{:S(2)}) collective-permute-start(bf16[320,512]{1,0:T(8,128)(2,1)S(1)} %bitcast.102), channel_id=1, source_target_pairs={{0,1},{1,2},{2,3},{3,0},{4,5},{5,6},{6,7},{7,4},{8,9},{9,10},{10,1... | collective-permute-start | bytes 983048 | tf_op jit(solution)/shard_map/ppermute | solution.py:262
  384.8 40.7 %collective-permute-start.24 = (bf16[320,512]{1,0:T(8,128)(2,1)S(1)}, bf16[320,512]{1,0:T(8,128)(2,1)S(1)}, u32[]{:S(2)}, u32[]{:S(2)}) collective-permute-start(bf16[320,512]{1,0:T(8,128)(2,1)S(1)} %bitcast.101), channel_id=1, source_target_pairs={{0,3},{1,0},{2,1},{3,2},{4,7},{5,4},{6,5},{7,6},{8,11},{9,8},{10,9... | collective-permute-start | bytes 983048 | tf_op jit(solution)/shard_map/ppermute | solution.py:262
  410.9 31.8 %collective-permute-start.25 = (bf16[320,512]{1,0:T(8,128)(2,1)S(1)}, bf16[320,512]{1,0:T(8,128)(2,1)S(1)}, u32[]{:S(2)}, u32[]{:S(2)}) collective-permute-start(bf16[320,512]{1,0:T(8,128)(2,1)S(1)} %bitcast.97), channel_id=1, source_target_pairs={{0,2},{1,3},{2,0},{3,1},{4,6},{5,7},{6,4},{7,5},{8,10},{9,11},{10,... | collective-permute-start | bytes 983048 | tf_op jit(solution)/shard_map/ppermute | solution.py:262
  421.7 25.4 %collective-permute-start.27 = (bf16[320,512]{1,0:T(8,128)(2,1)S(1)}, bf16[320,512]{1,0:T(8,128)(2,1)S(1)}, u32[]{:S(2)}, u32[]{:S(2)}) collective-permute-start(bf16[320,512]{1,0:T(8,128)(2,1)S(1)} %bitcast.110), channel_id=1, source_target_pairs={{0,3},{1,0},{2,1},{3,2},{4,7},{5,4},{6,5},{7,6},{8,11},{9,8},{10,9... | collective-permute-start | bytes 983048 | tf_op jit(solution)/shard_map/ppermute | solution.py:262
  425.5 43.6 %collective-permute-start.28 = (bf16[320,512]{1,0:T(8,128)(2,1)S(1)}, bf16[320,512]{1,0:T(8,128)(2,1)S(1)}, u32[]{:S(2)}, u32[]{:S(2)}) collective-permute-start(bf16[320,512]{1,0:T(8,128)(2,1)S(1)} %bitcast.108), channel_id=1, source_target_pairs={{0,2},{1,3},{2,0},{3,1},{4,6},{5,7},{6,4},{7,5},{8,10},{9,11},{10,... | collective-permute-start | bytes 983048 | tf_op jit(solution)/shard_map/ppermute | solution.py:262
  425.5 43.6 %collective-permute-start.29 = (bf16[320,512]{1,0:T(8,128)(2,1)S(1)}, bf16[320,512]{1,0:T(8,128)(2,1)S(1)}, u32[]{:S(2)}, u32[]{:S(2)}) collective-permute-start(bf16[320,512]{1,0:T(8,128)(2,1)S(1)} %bitcast.106), channel_id=1, source_target_pairs={{0,1},{1,2},{2,3},{3,0},{4,5},{5,6},{6,7},{7,4},{8,9},{9,10},{10,1... | collective-permute-start | bytes 983048 | tf_op jit(solution)/shard_map/ppermute | solution.py:262
  (48 other events, 601.7 us)
where the time goes:
time: 496 us; the launch traced here: 487 us
  waiting for transfers between devices  166 us (33%)
  starting transfers between devices  139 us (28%)
  Pallas kernels  135 us (27%)
  local copies, waits for them, and re-layouts  27.9 us (6%)
  other arithmetic  18.4 us (4%)
    ppermute x30, waiting for transfers between devices, across_planes(): lax.ppermute(parts[x], 'grp', [(p, (p + way * x) % planes) for p in range...  138 us
    ppermute x30, starting transfers between devices, across_planes(): lax.ppermute(parts[x], 'grp', [(p, (p + way * x) % planes) for p in range...  98.2 us
    pallas_call x5, Pallas kernels, longitudes(): pl.pallas_call(functools.partial(longitude_kernel, fields, 1.0 / math.sqr...  63.1 us
    all_to_all x10, starting transfers between devices, within_plane(): return lax.all_to_all(cut, 'band', split_axis=0, concat_axis=0, tiled=True)  40.4 us
    pallas_call x5, Pallas kernels, synthesize(): pl.pallas_call(functools.partial(synthesis_kernel, slots, levels, fields,...  32.7 us
    all_to_all x10, waiting for transfers between devices, within_plane(): return lax.all_to_all(cut, 'band', split_axis=0, concat_axis=0, tiled=True)  28 us
    pallas_call x5, Pallas kernels, fold(): pl.pallas_call(functools.partial(fold_kernel, slots, levels, fields), in_...  14.6 us
    pallas_call x1, Pallas kernels, analyze(): pl.pallas_call(functools.partial(analysis_kernel, len(folded), least), gr...  13.2 us
  transfers between devices with their start and end apart: 40, of which 18 were waited for; matrix products, arithmetic and copies ran while one was open for 5% of the time, Pallas kernels for 23%

commit v1 on v0

--- a/solution.py
+++ b/solution.py
@@ -256,17 +256,8 @@
     )(*parts, *[x.T for x in parts])
 
 
-def across_planes(parts, way):
-    planes = len(parts)
-    return [parts[0]] + [
-        lax.ppermute(parts[x], "grp", [(p, (p + way * x) % planes) for p in range(planes)]) for x in range(1, planes)
-    ]
-
-
-def within_plane(rows):
-    bands = lax.axis_size("band")
-    cut = rows.reshape(bands, -1, rows.shape[-1])
-    return lax.all_to_all(cut, "band", split_axis=0, concat_axis=0, tiled=True)
+def exchange(rows):
+    return lax.all_to_all(rows, AXES, split_axis=0, concat_axis=0, tiled=True)
 
 
 def after(value, *others):
@@ -289,51 +280,19 @@
     even = jnp.where(kept & ~is_odd, scale, 0.0).astype(jnp.float32)[:, None, :]
     odd = jnp.where(kept & is_odd, scale, 0.0).astype(jnp.float32)[:, None, :]
     spec_rows = spectral.reshape(slots, row_total, degrees)
-    planes, bands = lax.axis_size("grp"), lax.axis_size("band")
-    plane = lax.axis_index("grp")
-    sources = (plane + planes - jnp.arange(planes, dtype=jnp.int32)) % planes
-    owners = jnp.take(owner_table.reshape(bands, planes, slots), sources, axis=1).reshape(-1)
-    plane = plane.reshape(1)
-    least = tuple(4 * g * bands * planes for g in range(slots // 4))
+    least = tuple(8 * g * levels for g in range(slots // 4))
+    plane = jnp.zeros((1,), jnp.int32)
 
     def send(spec, tile):
-        return synthesize(plane, planes, spec, keep, flip, legendre, (tile, 1), fields, levels, least)
-
-    def stack(parts):
-        width = parts[0].shape[-1]
-        return jnp.stack([x.reshape(bands, -1, width) for x in parts], axis=1)
-
-    def give_back(cut, *others):
-        width = cut.shape[-1]
-        cut = cut.reshape(bands, planes, -1, width)
-        parts = [cut[:, x].reshape(-1, width) for x in range(planes)]
-        return across_planes(after(parts, *others), -1)
-
-    sent, moved, arrived, zonal, cuts, folded = [], [], [], [], [], []
-    for t in range(tiles + 2):
-        if t < tiles:
-            spec = spec_rows
-            if t == 1:
-                by_wave, by_lon = trig_tables(owners, lon_count)
-                spec = after(spec_rows, by_wave)
-            elif t >= 2:
-                spec = after(spec_rows, *moved[t - 2])
-            sent.append(send(spec, t))
-            moved.append(across_planes(sent[t], 1))
-        if t >= 1 and t - 1 < tiles:
-            ready = after(moved[t - 1], *sent[t]) if t < tiles else moved[t - 1]
-            if t >= 3:
-                ready = after(ready, cuts[t - 3])
-            arrived.append(within_plane(stack(ready)))
-        if t >= 2:
-            rows = arrived[t - 2]
-            values = longitudes(rows.reshape(-1, rows.shape[-1]), by_lon, by_wave, fields)
-            if t - 1 < tiles:
-                values = after(values, arrived[t - 1])
-            cuts.append(within_plane(values))
-    for t in range(tiles):
-        parts = give_back(cuts[t], *([folded[t - 2]] if t >= 2 else []))
-        folded.append(fold(plane, parts, slots, levels, fields))
+        return exchange(synthesize(plane, 1, spec, keep, flip, legendre, (tile, 1), fields, levels, least)[0])
+
+    arrived = [send(spec_rows, 0)]
+    by_wave, by_lon = trig_tables(owner_table, lon_count)
+    later = after(spec_rows, by_wave)
+    arrived += [send(later, tile) for tile in range(1, tiles)]
+    zonal = [longitudes(rows, by_lon, by_wave, fields) for rows in arrived]
+    returned = [exchange(rows) for rows in zonal]
+    folded = [fold(plane, [rows], slots, levels, fields) for rows in returned]
     out = analyze(folded, even, odd, legendre, row_total, least)
     return out.reshape(slots, 2, fields, levels, degrees)
 
@@ -411,9 +370,8 @@
 
 def on_device(spectral, legendre, owner_table):
     slots, _, _, levels, _ = spectral.shape
-    planes = lax.axis_size("grp")
-    whole_hemispheres = lax.axis_size("band") * planes == 2 * levels and planes & (planes - 1) == 0
-    if whole_hemispheres and legendre.shape[2] % LANES == 0 and slots % 4 == 0 and levels % 8 == 0:
+    whole_hemispheres = lax.axis_size("band") * lax.axis_size("grp") == 2 * levels
+    if whole_hemispheres and legendre.shape[2] % LANES == 0 and slots % 4 == 0 and levels % 16 == 0:
         return by_hemisphere_and_level(spectral, legendre, owner_table)
     return by_level_and_latitude(spectral, legendre, owner_table)
 

time: 496 us -> 418 us (0.84); the launches traced: 487 us -> 416 us
  starting transfers between devices: 139 us -> 48.6 us
  waiting for transfers between devices: 166 us -> 203 us
  local copies, waits for them, and re-layouts: 27.9 us -> 12.9 us
    all_to_all x10, waiting for transfers between devices: 28 us -> 203 us  [exchange(): return lax.all_to_all(rows, AXES, split_axis=0, concat_axis=0, tiled=True)]
    ppermute x30 -> x0, waiting for transfers between devices: 138 us -> none  [across_planes(): lax.ppermute(parts[x], 'grp', [(p, (p + way * x) % planes) for p in range...]
    ppermute x30 -> x0, starting transfers between devices: 98.2 us -> none  [across_planes(): lax.ppermute(parts[x], 'grp', [(p, (p + way * x) % planes) for p in range...]
    slice x5 -> x0, local copies, waits for them, and re-layouts: 8.13 us -> none  [give_back(): parts = [cut[:, x].reshape(-1, width) for x in range(planes)]]
    all_to_all x10, starting transfers between devices: 40.4 us -> 48.6 us  [exchange(): return lax.all_to_all(rows, AXES, split_axis=0, concat_axis=0, tiled=True)]
    another operation x5 -> x0, local copies, waits for them, and re-layouts: 6.07 us -> none  [stack(): return jnp.stack([x.reshape(bands, -1, width) for x in parts], axis=1)]
    unnamed x64 -> x20, local copies, waits for them, and re-layouts: 11.6 us -> 10.9 us
  transfers between devices with their start and end apart: 40 -> 10, of which waited for: 18 -> 10; matrix products, arithmetic and copies ran while one was open for 5% -> 0% of each run, Pallas kernels for 23% -> 24%
where the time goes in v1:
time: 418 us; the launch traced here: 416 us
  waiting for transfers between devices  203 us (49%)
  Pallas kernels  135 us (32%)
  starting transfers between devices  48.6 us (12%)
  other arithmetic  16.1 us (4%)
  local copies, waits for them, and re-layouts  12.9 us (3%)
    all_to_all x10, waiting for transfers between devices, exchange(): return lax.all_to_all(rows, AXES, split_axis=0, concat_axis=0, tiled=True)  203 us
    pallas_call x5, Pallas kernels, longitudes(): pl.pallas_call(functools.partial(longitude_kernel, fields, 1.0 / math.sqr...  63.2 us
    all_to_all x10, starting transfers between devices, exchange(): return lax.all_to_all(rows, AXES, split_axis=0, concat_axis=0, tiled=True)  48.6 us
    pallas_call x5, Pallas kernels, synthesize(): pl.pallas_call(functools.partial(synthesis_kernel, slots, levels, fields,...  32.4 us
    pallas_call x5, Pallas kernels, fold(): pl.pallas_call(functools.partial(fold_kernel, slots, levels, fields), in_...  14.8 us
    pallas_call x1, Pallas kernels, analyze(): pl.pallas_call(functools.partial(analysis_kernel, len(folded), least), gr...  13.2 us
    sin x4, other arithmetic, trig_tables(): parts = (jnp.cos(base), jnp.sin(base), jnp.cos(turn), jnp.sin(turn))  12.7 us
    pallas_call x1, Pallas kernels, trig_tables(): pl.pallas_call(trig_kernel, grid=(depth // rows,), in_specs=[small, small...  11.7 us
  transfers between devices with their start and end apart: 10, of which 10 were waited for; matrix products, arithmetic and copies ran while one was open for 0% of the time, Pallas kernels for 24%

profile of v1, /device:TPU:0, one launch (start us, length us, event | category | flops | bytes accessed | tf_op | source)
XLA Modules:
  0.0 415.5 jit_solution(13179654114933693128)
XLA Ops:
  17.1 11.7 %trig.1 = (bf16[1280,2560]{1,0:T(8,128)(2,1)}, bf16[2560,1280]{1,0:T(8,128)(2,1)}) custom-call(f32[1280,20]{1,0:T(8,128)} %get-tuple-element.14.cos_base_ref, f32[1280,20]{1,0:T(8,128)} %get-tuple-element.13.sin_base_ref, f32[1280,128]{1,0:T(8,128)} %get-tuple-element.18.cos_turn_ref, f32[1280,128]{1,0:T(8,128)} %get-tuple-element.17.sin_turn_ref, ...), custom_call_target="tpu_custom_call" | custom-call | flops 1000000 | bytes 10000 | tf_op jit(solution)/shard_map/trig/pallas_call | solution.py:241
  28.7 6.5 %synthesis.9 = bf16[1280,512]{1,0:T(8,128)(2,1)} custom-call(s32[1]{0:T(128)} %constant.17.clone.1.plane_ref, bf16[20,128,640]{2,1,0:T(8,128)(2,1)} %bitcast.22, bf16[20,1,640]{2,1,0:T(2,128)(2,1)} %fusion.11.keep_ref, bf16[20,1,640]{2,1,0:T(2,128)(2,1)} %negate_select_fusion.flip_ref, bf16[20,640,640]{2,1,0:T(8,128)(2,1)} %refs_7_.1), custom_call_target="tpu_custom_call" | custom-call | flops 1000000 | bytes 10000 | tf_op jit(solution)/shard_map/synthesis/pallas_call | solution.py:61
  35.3 7.3 %all-to-all-start.8 = ((bf16[32,40,512]{2,1,0:T(8,128)(2,1)}), bf16[32,40,512]{2,1,0:T(8,128)(2,1)S(1)}, u32[]{:S(2)}, u32[]{:S(2)}) async-start(bf16[32,40,512]{2,1,0:T(8,128)(2,1)} %bitcast.31), calls=%async_computation.8 | async-start | bytes 2621440 | tf_op jit(solution)/shard_map/all_to_all | solution.py:260
  42.6 6.5 %synthesis.8 = bf16[1280,512]{1,0:T(8,128)(2,1)} custom-call(s32[1]{0:T(128)} %constant.17.clone.1.plane_ref, bf16[20,128,640]{2,1,0:T(8,128)(2,1)} %bitcast.23, bf16[20,1,640]{2,1,0:T(2,128)(2,1)} %fusion.11.keep_ref, bf16[20,1,640]{2,1,0:T(2,128)(2,1)} %negate_select_fusion.flip_ref, bf16[20,640,640]{2,1,0:T(8,128)(2,1)} %refs_7_.1), custom_call_target="tpu_custom_call" | custom-call | flops 1000000 | bytes 10000 | tf_op jit(solution)/shard_map/synthesis/pallas_call | solution.py:61
  49.1 24.0 %all-to-all-done.8 = bf16[32,40,512]{2,1,0:T(8,128)(2,1)S(1)} async-done(((bf16[32,40,512]{2,1,0:T(8,128)(2,1)}), bf16[32,40,512]{2,1,0:T(8,128)(2,1)S(1)}, u32[]{:S(2)}, u32[]{:S(2)}) %all-to-all-start.8) | async-done | bytes 1310752 | tf_op jit(solution)/shard_map/all_to_all | solution.py:260
  78.8 6.5 %synthesis.7 = bf16[1280,512]{1,0:T(8,128)(2,1)} custom-call(s32[1]{0:T(128)} %constant.17.clone.1.plane_ref, bf16[20,128,640]{2,1,0:T(8,128)(2,1)} %bitcast.24, bf16[20,1,640]{2,1,0:T(2,128)(2,1)} %fusion.11.keep_ref, bf16[20,1,640]{2,1,0:T(2,128)(2,1)} %negate_select_fusion.flip_ref, bf16[20,640,640]{2,1,0:T(8,128)(2,1)} %refs_7_.1), custom_call_target="tpu_custom_call" | custom-call | flops 1000000 | bytes 10000 | tf_op jit(solution)/shard_map/synthesis/pallas_call | solution.py:61
  85.2 24.0 %all-to-all-done.6 = bf16[32,40,512]{2,1,0:T(8,128)(2,1)S(1)} async-done(((bf16[32,40,512]{2,1,0:T(8,128)(2,1)}), bf16[32,40,512]{2,1,0:T(8,128)(2,1)S(1)}, u32[]{:S(2)}, u32[]{:S(2)}) %all-to-all-start.6) | async-done | bytes 1310752 | tf_op jit(solution)/shard_map/all_to_all | solution.py:260
  115.1 6.4 %synthesis.6 = bf16[1280,512]{1,0:T(8,128)(2,1)} custom-call(s32[1]{0:T(128)} %constant.17.clone.1.plane_ref, bf16[20,128,640]{2,1,0:T(8,128)(2,1)} %bitcast.25, bf16[20,1,640]{2,1,0:T(2,128)(2,1)} %fusion.11.keep_ref, bf16[20,1,640]{2,1,0:T(2,128)(2,1)} %negate_select_fusion.flip_ref, bf16[20,640,640]{2,1,0:T(8,128)(2,1)} %refs_7_.1), custom_call_target="tpu_custom_call" | custom-call | flops 1000000 | bytes 10000 | tf_op jit(solution)/shard_map/synthesis/pallas_call | solution.py:61
  121.5 23.9 %all-to-all-done.4 = bf16[32,40,512]{2,1,0:T(8,128)(2,1)S(1)} async-done(((bf16[32,40,512]{2,1,0:T(8,128)(2,1)}), bf16[32,40,512]{2,1,0:T(8,128)(2,1)S(1)}, u32[]{:S(2)}, u32[]{:S(2)}) %all-to-all-start.4) | async-done | bytes 1310752 | tf_op jit(solution)/shard_map/all_to_all | solution.py:260
  151.0 6.5 %synthesis.5 = bf16[1280,512]{1,0:T(8,128)(2,1)} custom-call(s32[1]{0:T(128)} %constant.17.clone.1.plane_ref, bf16[20,128,640]{2,1,0:T(8,128)(2,1)} %bitcast.26, bf16[20,1,640]{2,1,0:T(2,128)(2,1)} %fusion.11.keep_ref, bf16[20,1,640]{2,1,0:T(2,128)(2,1)} %negate_select_fusion.flip_ref, bf16[20,640,640]{2,1,0:T(8,128)(2,1)} %refs_7_.1), custom_call_target="tpu_custom_call" | custom-call | flops 1000000 | bytes 10000 | tf_op jit(solution)/shard_map/synthesis/pallas_call | solution.py:61
  157.6 24.0 %all-to-all-done.2 = bf16[32,40,512]{2,1,0:T(8,128)(2,1)S(1)} async-done(((bf16[32,40,512]{2,1,0:T(8,128)(2,1)}), bf16[32,40,512]{2,1,0:T(8,128)(2,1)S(1)}, u32[]{:S(2)}, u32[]{:S(2)}) %all-to-all-start.2) | async-done | bytes 1310752 | tf_op jit(solution)/shard_map/all_to_all | solution.py:260
  187.1 12.7 %longitudes.9 = bf16[1280,512]{1,0:T(8,128)(2,1)} custom-call(bf16[1280,512]{1,0:T(8,128)(2,1)} %bitcast.41, bf16[2560,1280]{1,0:T(8,128)(2,1)} %get-tuple-element.8.by_lon_ref, bf16[1280,2560]{1,0:T(8,128)(2,1)} %get-tuple-element.9.by_wave_ref), custom_call_target="tpu_custom_call" | custom-call | flops 1000000 | bytes 10000 | tf_op jit(solution)/shard_map/longitudes/pallas_call | solution.py:107
  199.8 17.8 %all-to-all-done = bf16[32,40,512]{2,1,0:T(8,128)(2,1)S(1)} async-done(((bf16[32,40,512]{2,1,0:T(8,128)(2,1)}), bf16[32,40,512]{2,1,0:T(8,128)(2,1)S(1)}, u32[]{:S(2)}, u32[]{:S(2)}) %all-to-all-start) | async-done | bytes 1310752 | tf_op jit(solution)/shard_map/all_to_all | solution.py:260
  223.3 12.6 %longitudes.8 = bf16[1280,512]{1,0:T(8,128)(2,1)} custom-call(bf16[1280,512]{1,0:T(8,128)(2,1)} %bitcast.40, bf16[2560,1280]{1,0:T(8,128)(2,1)} %get-tuple-element.8.by_lon_ref, bf16[1280,2560]{1,0:T(8,128)(2,1)} %get-tuple-element.9.by_wave_ref), custom_call_target="tpu_custom_call" | custom-call | flops 1000000 | bytes 10000 | tf_op jit(solution)/shard_map/longitudes/pallas_call | solution.py:107
  235.9 17.9 %all-to-all-done.9 = bf16[32,40,512]{2,1,0:T(8,128)(2,1)S(1)} async-done(((bf16[32,40,512]{2,1,0:T(8,128)(2,1)}), bf16[32,40,512]{2,1,0:T(8,128)(2,1)S(1)}, u32[]{:S(2)}, u32[]{:S(2)}) %all-to-all-start.9) | async-done | bytes 1310752 | tf_op jit(solution)/shard_map/all_to_all | solution.py:260
  259.4 12.7 %longitudes.7 = bf16[1280,512]{1,0:T(8,128)(2,1)} custom-call(bf16[1280,512]{1,0:T(8,128)(2,1)} %bitcast.39, bf16[2560,1280]{1,0:T(8,128)(2,1)} %get-tuple-element.8.by_lon_ref, bf16[1280,2560]{1,0:T(8,128)(2,1)} %get-tuple-element.9.by_wave_ref), custom_call_target="tpu_custom_call" | custom-call | flops 1000000 | bytes 10000 | tf_op jit(solution)/shard_map/longitudes/pallas_call | solution.py:107
  272.1 17.8 %all-to-all-done.7 = bf16[32,40,512]{2,1,0:T(8,128)(2,1)S(1)} async-done(((bf16[32,40,512]{2,1,0:T(8,128)(2,1)}), bf16[32,40,512]{2,1,0:T(8,128)(2,1)S(1)}, u32[]{:S(2)}, u32[]{:S(2)}) %all-to-all-start.7) | async-done | bytes 1310752 | tf_op jit(solution)/shard_map/all_to_all | solution.py:260
  295.6 12.6 %longitudes.6 = bf16[1280,512]{1,0:T(8,128)(2,1)} custom-call(bf16[1280,512]{1,0:T(8,128)(2,1)} %bitcast.38, bf16[2560,1280]{1,0:T(8,128)(2,1)} %get-tuple-element.8.by_lon_ref, bf16[1280,2560]{1,0:T(8,128)(2,1)} %get-tuple-element.9.by_wave_ref), custom_call_target="tpu_custom_call" | custom-call | flops 1000000 | bytes 10000 | tf_op jit(solution)/shard_map/longitudes/pallas_call | solution.py:107
  308.2 17.9 %all-to-all-done.5 = bf16[32,40,512]{2,1,0:T(8,128)(2,1)S(1)} async-done(((bf16[32,40,512]{2,1,0:T(8,128)(2,1)}), bf16[32,40,512]{2,1,0:T(8,128)(2,1)S(1)}, u32[]{:S(2)}, u32[]{:S(2)}) %all-to-all-start.5) | async-done | bytes 1310752 | tf_op jit(solution)/shard_map/all_to_all | solution.py:260
  327.2 4.8 %all-to-all-start.3 = ((bf16[32,40,512]{2,1,0:T(8,128)(2,1)}), bf16[32,40,512]{2,1,0:T(8,128)(2,1)S(1)}, u32[]{:S(2)}, u32[]{:S(2)}) async-start(bf16[32,40,512]{2,1,0:T(8,128)(2,1)} %bitcast.43), calls=%async_computation.3 | async-start | bytes 2621440 | tf_op jit(solution)/shard_map/all_to_all | solution.py:260
  332.0 12.6 %longitudes.5 = bf16[1280,512]{1,0:T(8,128)(2,1)} custom-call(bf16[1280,512]{1,0:T(8,128)(2,1)} %bitcast.37, bf16[2560,1280]{1,0:T(8,128)(2,1)} %get-tuple-element.8.by_lon_ref, bf16[1280,2560]{1,0:T(8,128)(2,1)} %get-tuple-element.9.by_wave_ref), custom_call_target="tpu_custom_call" | custom-call | flops 1000000 | bytes 10000 | tf_op jit(solution)/shard_map/longitudes/pallas_call | solution.py:107
  344.6 17.6 %all-to-all-done.3 = bf16[32,40,512]{2,1,0:T(8,128)(2,1)S(1)} async-done(((bf16[32,40,512]{2,1,0:T(8,128)(2,1)}), bf16[32,40,512]{2,1,0:T(8,128)(2,1)S(1)}, u32[]{:S(2)}, u32[]{:S(2)}) %all-to-all-start.3) | async-done | bytes 1310752 | tf_op jit(solution)/shard_map/all_to_all | solution.py:260
  380.8 17.6 %all-to-all-done.1 = bf16[32,40,512]{2,1,0:T(8,128)(2,1)S(1)} async-done(((bf16[32,40,512]{2,1,0:T(8,128)(2,1)}), bf16[32,40,512]{2,1,0:T(8,128)(2,1)S(1)}, u32[]{:S(2)}, u32[]{:S(2)}) %all-to-all-start.1) | async-done | bytes 1310752 | tf_op jit(solution)/shard_map/all_to_all | solution.py:260
  402.4 13.2 %analysis.1 = f32[20,128,640]{2,1,0:T(8,128)} custom-call(bf16[20,256,128]{2,1,0:T(8,128)(2,1)} %fold.5.refs_0_, bf16[20,256,128]{2,1,0:T(8,128)(2,1)} %fold.6.refs_1_, bf16[20,256,128]{2,1,0:T(8,128)(2,1)} %fold.7.refs_2_, bf16[20,256,128]{2,1,0:T(8,128)(2,1)} %fold.8.refs_3_, bf16[20,256,128]{2,1,0:T(8,128)(2,1)} %fold.9.refs_4_, ...), custom_call_target="tpu_custom_call" | custom-call | flops 4194304000 | bytes 29491200 | tf_op jit(solution)/shard_map/analysis/pallas_call | solution.py:194
  (47 shorter events, 80.3 us)
Async XLA Ops:
  35.3 37.8 %all-to-all-start.8 = ((bf16[32,40,512]{2,1,0:T(8,128)(2,1)}), bf16[32,40,512]{2,1,0:T(8,128)(2,1)S(1)}, u32[]{:S(2)}, u32[]{:S(2)}) async-start(bf16[32,40,512]{2,1,0:T(8,128)(2,1)} %bitcast.31), calls=%async_computation.8 | async-start | bytes 2621440 | tf_op jit(solution)/shard_map/all_to_all | solution.py:260
  73.1 1.1 copy-start.9
  74.2 35.0 %all-to-all-start.6 = ((bf16[32,40,512]{2,1,0:T(8,128)(2,1)}), bf16[32,40,512]{2,1,0:T(8,128)(2,1)S(1)}, u32[]{:S(2)}, u32[]{:S(2)}) async-start(bf16[32,40,512]{2,1,0:T(8,128)(2,1)} %bitcast.29), calls=%async_computation.6 | async-start | bytes 2621440 | tf_op jit(solution)/shard_map/all_to_all | solution.py:260
  109.3 1.1 copy-start.8
  110.3 35.0 %all-to-all-start.4 = ((bf16[32,40,512]{2,1,0:T(8,128)(2,1)}), bf16[32,40,512]{2,1,0:T(8,128)(2,1)S(1)}, u32[]{:S(2)}, u32[]{:S(2)}) async-start(bf16[32,40,512]{2,1,0:T(8,128)(2,1)} %bitcast.30), calls=%async_computation.4 | async-start | bytes 2621440 | tf_op jit(solution)/shard_map/all_to_all | solution.py:260
  145.4 1.1 copy-start.7
  146.5 35.0 %all-to-all-start.2 = ((bf16[32,40,512]{2,1,0:T(8,128)(2,1)}), bf16[32,40,512]{2,1,0:T(8,128)(2,1)S(1)}, u32[]{:S(2)}, u32[]{:S(2)}) async-start(bf16[32,40,512]{2,1,0:T(8,128)(2,1)} %bitcast.28), calls=%async_computation.2 | async-start | bytes 2621440 | tf_op jit(solution)/shard_map/all_to_all | solution.py:260
  181.5 1.0 copy-start.6
  182.6 35.0 %all-to-all-start = ((bf16[32,40,512]{2,1,0:T(8,128)(2,1)}), bf16[32,40,512]{2,1,0:T(8,128)(2,1)S(1)}, u32[]{:S(2)}, u32[]{:S(2)}) async-start(bf16[32,40,512]{2,1,0:T(8,128)(2,1)} %bitcast.27), calls=%async_computation | async-start | bytes 2621440 | tf_op jit(solution)/shard_map/all_to_all | solution.py:260
  217.6 1.1 copy-start.5
  218.8 35.0 %all-to-all-start.9 = ((bf16[32,40,512]{2,1,0:T(8,128)(2,1)}), bf16[32,40,512]{2,1,0:T(8,128)(2,1)S(1)}, u32[]{:S(2)}, u32[]{:S(2)}) async-start(bf16[32,40,512]{2,1,0:T(8,128)(2,1)} %bitcast.44), calls=%async_computation.9 | async-start | bytes 2621440 | tf_op jit(solution)/shard_map/all_to_all | solution.py:260
  253.8 1.1 copy-start
  254.9 35.0 %all-to-all-start.7 = ((bf16[32,40,512]{2,1,0:T(8,128)(2,1)}), bf16[32,40,512]{2,1,0:T(8,128)(2,1)S(1)}, u32[]{:S(2)}, u32[]{:S(2)}) async-start(bf16[32,40,512]{2,1,0:T(8,128)(2,1)} %bitcast.45), calls=%async_computation.7 | async-start | bytes 2621440 | tf_op jit(solution)/shard_map/all_to_all | solution.py:260
  289.9 1.1 copy-start.1
  291.0 35.0 %all-to-all-start.5 = ((bf16[32,40,512]{2,1,0:T(8,128)(2,1)}), bf16[32,40,512]{2,1,0:T(8,128)(2,1)S(1)}, u32[]{:S(2)}, u32[]{:S(2)}) async-start(bf16[32,40,512]{2,1,0:T(8,128)(2,1)} %bitcast.46), calls=%async_computation.5 | async-start | bytes 2621440 | tf_op jit(solution)/shard_map/all_to_all | solution.py:260
  326.1 1.1 copy-start.2
  327.2 35.0 %all-to-all-start.3 = ((bf16[32,40,512]{2,1,0:T(8,128)(2,1)}), bf16[32,40,512]{2,1,0:T(8,128)(2,1)S(1)}, u32[]{:S(2)}, u32[]{:S(2)}) async-start(bf16[32,40,512]{2,1,0:T(8,128)(2,1)} %bitcast.43), calls=%async_computation.3 | async-start | bytes 2621440 | tf_op jit(solution)/shard_map/all_to_all | solution.py:260
  362.3 1.1 copy-start.3
  363.3 35.0 %all-to-all-start.1 = ((bf16[32,40,512]{2,1,0:T(8,128)(2,1)}), bf16[32,40,512]{2,1,0:T(8,128)(2,1)S(1)}, u32[]{:S(2)}, u32[]{:S(2)}) async-start(bf16[32,40,512]{2,1,0:T(8,128)(2,1)} %bitcast.42), calls=%async_computation.1 | async-start | bytes 2621440 | tf_op jit(solution)/shard_map/all_to_all | solution.py:260
  398.4 1.1 copy-start.4

commit v2 on v1

--- a/solution.py
+++ b/solution.py
@@ -11,7 +11,6 @@
 LANES = 128
 AXES = ("band", "grp")
 VMEM_BYTES = 56 * 1024 * 1024
-BRIEF = pl.CostEstimate(flops=10**6, bytes_accessed=10**4, transcendentals=0)
 
 
 def synthesis_kernel(slots, levels, fields, least, scale, plane_ref, spec_ref, keep_ref, flip_ref, table_ref, *refs):
@@ -74,7 +73,11 @@
         ),
         out_shape=[jax.ShapeDtypeStruct(shape, jnp.bfloat16)] * planes,
         compiler_params=pltpu.CompilerParams(vmem_limit_bytes=VMEM_BYTES),
-        cost_estimate=BRIEF,
+        cost_estimate=pl.CostEstimate(
+            flops=4 * slots * row_total * degrees * tiles * LANES,
+            bytes_accessed=2 * slots * degrees * (row_total + tiles * LANES) + 2 * rows * shape[1],
+            transcendentals=0,
+        ),
         name="synthesis",
     )(plane, spec_rows, keep, flip, legendre)
 
@@ -116,7 +119,11 @@
         out_shape=jax.ShapeDtypeStruct((depth, width), jnp.bfloat16),
         scratch_shapes=[pltpu.VMEM((depth, width), jnp.float32)],
         compiler_params=pltpu.CompilerParams(vmem_limit_bytes=VMEM_BYTES),
-        cost_estimate=BRIEF,
+        cost_estimate=pl.CostEstimate(
+            flops=4 * depth * width * lon_count,
+            bytes_accessed=4 * depth * (width + lon_count),
+            transcendentals=0,
+        ),
         name="longitudes",
     )(rows, by_lon, by_wave)
 
@@ -160,14 +167,15 @@
         out_shape=jax.ShapeDtypeStruct(shape, jnp.bfloat16),
         scratch_shapes=[pltpu.VMEM((fields, tiles, rows, LANES), jnp.float32)],
         compiler_params=pltpu.CompilerParams(vmem_limit_bytes=VMEM_BYTES),
-        cost_estimate=BRIEF,
+        cost_estimate=pl.CostEstimate(flops=2 * size, bytes_accessed=4 * size, transcendentals=0),
         name="fold",
     )(plane, *parts)
 
 
-def analysis_kernel(chunks, least, *refs):
+def analysis_kernel(chunks, least, adds, *refs):
     folded_refs = refs[:chunks]
-    even_ref, odd_ref, table_ref, out_ref = refs[chunks:]
+    even_ref, odd_ref, table_ref = refs[chunks : chunks + 3]
+    base_ref, out_ref = refs[-2], refs[-1]
     row_total, degrees = out_ref.shape[1:]
     step = pl.program_id(0)
 
@@ -179,6 +187,8 @@
                 folded, table_ref[j, start:, :], (((1,), (1,)), ((), ())), preferred_element_type=jnp.float32
             )
             kept = sums[:row_total] * even_ref[j, :, start:] + sums[row_total:] * odd_ref[j, :, start:]
+            if adds:
+                kept = kept + base_ref[j, :, start:]
             out_ref[j, :, start:] = kept
             if start:
                 out_ref[j, :, :start] = jnp.zeros((row_total, start), out_ref.dtype)
@@ -187,16 +197,20 @@
         pl.when(step == group)(functools.partial(run, group))
 
 
-def analyze(folded, even, odd, legendre, row_total, least):
-    slots, degrees, lat_count = legendre.shape
+def analyze(folded, even, odd, legendre, row_total, least, first_tile, base=None):
+    slots, degrees, _ = legendre.shape
     block = slots // len(least)
+    lat_count = len(folded) * LANES
+    table_block = first_tile // len(folded)
     mask_spec = pl.BlockSpec((block, 1, degrees), lambda i: (i, 0, 0))
+    sums_spec = pl.BlockSpec((block, row_total, degrees), lambda i: (i, 0, 0))
     return pl.pallas_call(
-        functools.partial(analysis_kernel, len(folded), least),
+        functools.partial(analysis_kernel, len(folded), least, base is not None),
         grid=(len(least),),
         in_specs=[pl.BlockSpec((block,) + x.shape[1:], lambda i: (i, 0, 0)) for x in folded]
-        + [mask_spec, mask_spec, pl.BlockSpec((block, degrees, lat_count), lambda i: (i, 0, 0))],
-        out_specs=pl.BlockSpec((block, row_total, degrees), lambda i: (i, 0, 0)),
+        + [mask_spec, mask_spec, pl.BlockSpec((block, degrees, lat_count), lambda i: (i, 0, table_block))]
+        + ([sums_spec] if base is not None else []),
+        out_specs=sums_spec,
         out_shape=jax.ShapeDtypeStruct((slots, row_total, degrees), jnp.float32),
         compiler_params=pltpu.CompilerParams(vmem_limit_bytes=VMEM_BYTES),
         cost_estimate=pl.CostEstimate(
@@ -205,7 +219,7 @@
             transcendentals=0,
         ),
         name="analysis",
-    )(*folded, even, odd, legendre)
+    )(*folded, even, odd, legendre, *([base] if base is not None else []))
 
 
 def trig_kernel(cos_base_ref, sin_base_ref, cos_turn_ref, sin_turn_ref, cos_base_t, sin_base_t, cos_turn_t, sin_turn_t, by_wave_ref, by_lon_ref):
@@ -251,7 +265,9 @@
             jax.ShapeDtypeStruct((lon_count, depth), jnp.bfloat16),
         ],
         compiler_params=pltpu.CompilerParams(vmem_limit_bytes=VMEM_BYTES),
-        cost_estimate=BRIEF,
+        cost_estimate=pl.CostEstimate(
+            flops=8 * depth * lon_count, bytes_accessed=4 * depth * lon_count, transcendentals=0
+        ),
         name="trig",
     )(*parts, *[x.T for x in parts])
 
@@ -284,16 +300,18 @@
     plane = jnp.zeros((1,), jnp.int32)
 
     def send(spec, tile):
-        return exchange(synthesize(plane, 1, spec, keep, flip, legendre, (tile, 1), fields, levels, least)[0])
-
-    arrived = [send(spec_rows, 0)]
-    by_wave, by_lon = trig_tables(owner_table, lon_count)
+        return synthesize(plane, 1, spec, keep, flip, legendre, (tile, 1), fields, levels, least)[0]
+
+    sent = [send(spec_rows, 0)]
+    by_wave, by_lon = trig_tables(after(owner_table, sent[0]), lon_count)
     later = after(spec_rows, by_wave)
-    arrived += [send(later, tile) for tile in range(1, tiles)]
+    sent += [send(later, tile) for tile in range(1, tiles)]
+    arrived = [exchange(rows) for rows in sent]
     zonal = [longitudes(rows, by_lon, by_wave, fields) for rows in arrived]
     returned = [exchange(rows) for rows in zonal]
     folded = [fold(plane, [rows], slots, levels, fields) for rows in returned]
-    out = analyze(folded, even, odd, legendre, row_total, least)
+    base = analyze(folded[:-1], even, odd, legendre, row_total, least, 0)
+    out = analyze(folded[-1:], even, odd, legendre, row_total, least, tiles - 1, base)
     return out.reshape(slots, 2, fields, levels, degrees)
 
 

time: 418 us -> 402 us (0.962)
  waiting for transfers between devices: 203 us -> 179 us
  Pallas kernels: 135 us -> 143 us
    all_to_all x10, waiting for transfers between devices: 203 us -> 179 us  [exchange(): return lax.all_to_all(rows, AXES, split_axis=0, concat_axis=0, tiled=True)]
    pallas_call x1 -> x2, Pallas kernels: 13.2 us -> 20.8 us  [analyze(): pl.pallas_call(functools.partial(analysis_kernel, len(folded), least, bas...]
    unnamed x20 -> x24, local copies, waits for them, and re-layouts: 10.9 us -> 10.9 us
  transfers between devices with their start and end apart: 10 -> 10, of which waited for: 10 -> 9; matrix products, arithmetic and copies ran while one was open for 0% -> 4% of each run, Pallas kernels for 24% -> 28%
where the time goes in v2:
time: 402 us; the launch traced here: 399 us
  waiting for transfers between devices  179 us (45%)
  Pallas kernels  143 us (36%)
  starting transfers between devices  49.8 us (12%)
  other arithmetic  15.2 us (4%)
  local copies, waits for them, and re-layouts  12.3 us (3%)
    all_to_all x10, waiting for transfers between devices, exchange(): return lax.all_to_all(rows, AXES, split_axis=0, concat_axis=0, tiled=True)  179 us
    pallas_call x5, Pallas kernels, longitudes(): pl.pallas_call(functools.partial(longitude_kernel, fields, 1.0 / math.sqr...  63.2 us
    all_to_all x10, starting transfers between devices, exchange(): return lax.all_to_all(rows, AXES, split_axis=0, concat_axis=0, tiled=True)  49.8 us
    pallas_call x5, Pallas kernels, synthesize(): pl.pallas_call(functools.partial(synthesis_kernel, slots, levels, fields,...  32.3 us
    pallas_call x2, Pallas kernels, analyze(): pl.pallas_call(functools.partial(analysis_kernel, len(folded), least, bas...  20.8 us
    pallas_call x5, Pallas kernels, fold(): pl.pallas_call(functools.partial(fold_kernel, slots, levels, fields), in_...  14.9 us
    sin x4, other arithmetic, trig_tables(): parts = (jnp.cos(base), jnp.sin(base), jnp.cos(turn), jnp.sin(turn))  12.5 us
    pallas_call x1, Pallas kernels, trig_tables(): pl.pallas_call(trig_kernel, grid=(depth // rows,), in_specs=[small, small...  11.8 us
  transfers between devices with their start and end apart: 10, of which 9 were waited for; matrix products, arithmetic and copies ran while one was open for 4% of the time, Pallas kernels for 28%

profile of v2, /device:TPU:0, one launch (start us, length us, event | category | flops | bytes accessed | tf_op | source)
XLA Modules:
  0.0 399.0 jit_solution(15541827780147536463)
XLA Ops:
  2.4 6.5 %synthesis.5 = bf16[1280,512]{1,0:T(8,128)(2,1)} custom-call(s32[1]{0:T(128)} %constant.17.clone.1.plane_ref, bf16[20,128,640]{2,1,0:T(8,128)(2,1)} %bitcast.22, bf16[20,1,640]{2,1,0:T(2,128)(2,1)} %fusion.11.keep_ref, bf16[20,1,640]{2,1,0:T(2,128)(2,1)} %negate_select_fusion.flip_ref, bf16[20,640,640]{2,1,0:T(8,128)(2,1)} %refs_3_.1), custom_call_target="tpu_custom_call" | custom-call | flops 838860800 | bytes 7864320 | tf_op jit(solution)/shard_map/synthesis/pallas_call | solution.py:60
  8.9 7.3 %all-to-all-start.2 = ((bf16[32,40,512]{2,1,0:T(8,128)(2,1)}), bf16[32,40,512]{2,1,0:T(8,128)(2,1)S(1)}, u32[]{:S(2)}, u32[]{:S(2)}) async-start(bf16[32,40,512]{2,1,0:T(8,128)(2,1)} %bitcast.27), calls=%async_computation.2 | async-start | bytes 2621440 | tf_op jit(solution)/shard_map/all_to_all | solution.py:276
  29.4 11.8 %trig.1 = (bf16[1280,2560]{1,0:T(8,128)(2,1)}, bf16[2560,1280]{1,0:T(8,128)(2,1)}) custom-call(f32[1280,20]{1,0:T(8,128)} %get-tuple-element.16.cos_base_ref, f32[1280,20]{1,0:T(8,128)} %get-tuple-element.15.sin_base_ref, f32[1280,128]{1,0:T(8,128)} %get-tuple-element.20.cos_turn_ref, f32[1280,128]{1,0:T(8,128)} %get-tuple-element.19.sin_turn_ref, ...), custom_call_target="tpu_custom_call" | custom-call | flops 26214400 | bytes 13107200 | tf_op jit(solution)/shard_map/trig/pallas_call | solution.py:255
  41.1 6.4 %synthesis.9 = bf16[1280,512]{1,0:T(8,128)(2,1)} custom-call(s32[1]{0:T(128)} %constant.17.clone.1.plane_ref, bf16[20,128,640]{2,1,0:T(8,128)(2,1)} %bitcast.23, bf16[20,1,640]{2,1,0:T(2,128)(2,1)} %fusion.11.keep_ref, bf16[20,1,640]{2,1,0:T(2,128)(2,1)} %negate_select_fusion.flip_ref, bf16[20,640,640]{2,1,0:T(8,128)(2,1)} %refs_3_.1), custom_call_target="tpu_custom_call" | custom-call | flops 838860800 | bytes 7864320 | tf_op jit(solution)/shard_map/synthesis/pallas_call | solution.py:60
  48.7 5.8 %all-to-all-start.8 = ((bf16[32,40,512]{2,1,0:T(8,128)(2,1)}), bf16[32,40,512]{2,1,0:T(8,128)(2,1)S(1)}, u32[]{:S(2)}, u32[]{:S(2)}) async-start(bf16[32,40,512]{2,1,0:T(8,128)(2,1)} %bitcast.30), calls=%async_computation.8 | async-start | bytes 2621440 | tf_op jit(solution)/shard_map/all_to_all | solution.py:276
  54.6 6.5 %synthesis.8 = bf16[1280,512]{1,0:T(8,128)(2,1)} custom-call(s32[1]{0:T(128)} %constant.17.clone.1.plane_ref, bf16[20,128,640]{2,1,0:T(8,128)(2,1)} %bitcast.24, bf16[20,1,640]{2,1,0:T(2,128)(2,1)} %fusion.11.keep_ref, bf16[20,1,640]{2,1,0:T(2,128)(2,1)} %negate_select_fusion.flip_ref, bf16[20,640,640]{2,1,0:T(8,128)(2,1)} %refs_3_.1), custom_call_target="tpu_custom_call" | custom-call | flops 838860800 | bytes 7864320 | tf_op jit(solution)/shard_map/synthesis/pallas_call | solution.py:60
  61.1 24.0 %all-to-all-done.8 = bf16[32,40,512]{2,1,0:T(8,128)(2,1)S(1)} async-done(((bf16[32,40,512]{2,1,0:T(8,128)(2,1)}), bf16[32,40,512]{2,1,0:T(8,128)(2,1)S(1)}, u32[]{:S(2)}, u32[]{:S(2)}) %all-to-all-start.8) | async-done | bytes 1310752 | tf_op jit(solution)/shard_map/all_to_all | solution.py:276
  90.9 6.4 %synthesis.7 = bf16[1280,512]{1,0:T(8,128)(2,1)} custom-call(s32[1]{0:T(128)} %constant.17.clone.1.plane_ref, bf16[20,128,640]{2,1,0:T(8,128)(2,1)} %bitcast.25, bf16[20,1,640]{2,1,0:T(2,128)(2,1)} %fusion.11.keep_ref, bf16[20,1,640]{2,1,0:T(2,128)(2,1)} %negate_select_fusion.flip_ref, bf16[20,640,640]{2,1,0:T(8,128)(2,1)} %refs_3_.1), custom_call_target="tpu_custom_call" | custom-call | flops 838860800 | bytes 7864320 | tf_op jit(solution)/shard_map/synthesis/pallas_call | solution.py:60
  97.3 23.9 %all-to-all-done.6 = bf16[32,40,512]{2,1,0:T(8,128)(2,1)S(1)} async-done(((bf16[32,40,512]{2,1,0:T(8,128)(2,1)}), bf16[32,40,512]{2,1,0:T(8,128)(2,1)S(1)}, u32[]{:S(2)}, u32[]{:S(2)}) %all-to-all-start.6) | async-done | bytes 1310752 | tf_op jit(solution)/shard_map/all_to_all | solution.py:276
  126.8 6.5 %synthesis.6 = bf16[1280,512]{1,0:T(8,128)(2,1)} custom-call(s32[1]{0:T(128)} %constant.17.clone.1.plane_ref, bf16[20,128,640]{2,1,0:T(8,128)(2,1)} %bitcast.26, bf16[20,1,640]{2,1,0:T(2,128)(2,1)} %fusion.11.keep_ref, bf16[20,1,640]{2,1,0:T(2,128)(2,1)} %negate_select_fusion.flip_ref, bf16[20,640,640]{2,1,0:T(8,128)(2,1)} %refs_3_.1), custom_call_target="tpu_custom_call" | custom-call | flops 838860800 | bytes 7864320 | tf_op jit(solution)/shard_map/synthesis/pallas_call | solution.py:60
  133.4 24.0 %all-to-all-done.4 = bf16[32,40,512]{2,1,0:T(8,128)(2,1)S(1)} async-done(((bf16[32,40,512]{2,1,0:T(8,128)(2,1)}), bf16[32,40,512]{2,1,0:T(8,128)(2,1)S(1)}, u32[]{:S(2)}, u32[]{:S(2)}) %all-to-all-start.4) | async-done | bytes 1310752 | tf_op jit(solution)/shard_map/all_to_all | solution.py:276
  162.9 12.6 %longitudes.6 = bf16[1280,512]{1,0:T(8,128)(2,1)} custom-call(bf16[1280,512]{1,0:T(8,128)(2,1)} %bitcast.37, bf16[2560,1280]{1,0:T(8,128)(2,1)} %get-tuple-element.12.by_lon_ref, bf16[1280,2560]{1,0:T(8,128)(2,1)} %get-tuple-element.10.by_wave_ref), custom_call_target="tpu_custom_call" | custom-call | flops 6710886400 | bytes 15728640 | tf_op jit(solution)/shard_map/longitudes/pallas_call | solution.py:110
  175.6 17.9 %all-to-all-done = bf16[32,40,512]{2,1,0:T(8,128)(2,1)S(1)} async-done(((bf16[32,40,512]{2,1,0:T(8,128)(2,1)}), bf16[32,40,512]{2,1,0:T(8,128)(2,1)S(1)}, u32[]{:S(2)}, u32[]{:S(2)}) %all-to-all-start) | async-done | bytes 1310752 | tf_op jit(solution)/shard_map/all_to_all | solution.py:276
  199.1 12.6 %longitudes.9 = bf16[1280,512]{1,0:T(8,128)(2,1)} custom-call(bf16[1280,512]{1,0:T(8,128)(2,1)} %bitcast.41, bf16[2560,1280]{1,0:T(8,128)(2,1)} %get-tuple-element.12.by_lon_ref, bf16[1280,2560]{1,0:T(8,128)(2,1)} %get-tuple-element.10.by_wave_ref), custom_call_target="tpu_custom_call" | custom-call | flops 6710886400 | bytes 15728640 | tf_op jit(solution)/shard_map/longitudes/pallas_call | solution.py:110
  211.8 17.9 %all-to-all-done.3 = bf16[32,40,512]{2,1,0:T(8,128)(2,1)S(1)} async-done(((bf16[32,40,512]{2,1,0:T(8,128)(2,1)}), bf16[32,40,512]{2,1,0:T(8,128)(2,1)S(1)}, u32[]{:S(2)}, u32[]{:S(2)}) %all-to-all-start.3) | async-done | bytes 1310752 | tf_op jit(solution)/shard_map/all_to_all | solution.py:276
  235.3 12.7 %longitudes.8 = bf16[1280,512]{1,0:T(8,128)(2,1)} custom-call(bf16[1280,512]{1,0:T(8,128)(2,1)} %bitcast.40, bf16[2560,1280]{1,0:T(8,128)(2,1)} %get-tuple-element.12.by_lon_ref, bf16[1280,2560]{1,0:T(8,128)(2,1)} %get-tuple-element.10.by_wave_ref), custom_call_target="tpu_custom_call" | custom-call | flops 6710886400 | bytes 15728640 | tf_op jit(solution)/shard_map/longitudes/pallas_call | solution.py:110
  248.0 17.8 %all-to-all-done.9 = bf16[32,40,512]{2,1,0:T(8,128)(2,1)S(1)} async-done(((bf16[32,40,512]{2,1,0:T(8,128)(2,1)}), bf16[32,40,512]{2,1,0:T(8,128)(2,1)S(1)}, u32[]{:S(2)}, u32[]{:S(2)}) %all-to-all-start.9) | async-done | bytes 1310752 | tf_op jit(solution)/shard_map/all_to_all | solution.py:276
  271.4 12.6 %longitudes.7 = bf16[1280,512]{1,0:T(8,128)(2,1)} custom-call(bf16[1280,512]{1,0:T(8,128)(2,1)} %bitcast.39, bf16[2560,1280]{1,0:T(8,128)(2,1)} %get-tuple-element.12.by_lon_ref, bf16[1280,2560]{1,0:T(8,128)(2,1)} %get-tuple-element.10.by_wave_ref), custom_call_target="tpu_custom_call" | custom-call | flops 6710886400 | bytes 15728640 | tf_op jit(solution)/shard_map/longitudes/pallas_call | solution.py:110
  284.0 17.9 %all-to-all-done.7 = bf16[32,40,512]{2,1,0:T(8,128)(2,1)S(1)} async-done(((bf16[32,40,512]{2,1,0:T(8,128)(2,1)}), bf16[32,40,512]{2,1,0:T(8,128)(2,1)S(1)}, u32[]{:S(2)}, u32[]{:S(2)}) %all-to-all-start.7) | async-done | bytes 1310752 | tf_op jit(solution)/shard_map/all_to_all | solution.py:276
  307.8 12.6 %longitudes.5 = bf16[1280,512]{1,0:T(8,128)(2,1)} custom-call(bf16[1280,512]{1,0:T(8,128)(2,1)} %bitcast.38, bf16[2560,1280]{1,0:T(8,128)(2,1)} %get-tuple-element.12.by_lon_ref, bf16[1280,2560]{1,0:T(8,128)(2,1)} %get-tuple-element.10.by_wave_ref), custom_call_target="tpu_custom_call" | custom-call | flops 6710886400 | bytes 15728640 | tf_op jit(solution)/shard_map/longitudes/pallas_call | solution.py:110
  320.4 17.7 %all-to-all-done.5 = bf16[32,40,512]{2,1,0:T(8,128)(2,1)S(1)} async-done(((bf16[32,40,512]{2,1,0:T(8,128)(2,1)}), bf16[32,40,512]{2,1,0:T(8,128)(2,1)S(1)}, u32[]{:S(2)}, u32[]{:S(2)}) %all-to-all-start.5) | async-done | bytes 1310752 | tf_op jit(solution)/shard_map/all_to_all | solution.py:276
  356.6 17.6 %all-to-all-done.1 = bf16[32,40,512]{2,1,0:T(8,128)(2,1)S(1)} async-done(((bf16[32,40,512]{2,1,0:T(8,128)(2,1)}), bf16[32,40,512]{2,1,0:T(8,128)(2,1)S(1)}, u32[]{:S(2)}, u32[]{:S(2)}) %all-to-all-start.1) | async-done | bytes 1310752 | tf_op jit(solution)/shard_map/all_to_all | solution.py:276
  378.2 11.6 %analysis.2.refs_4_ = f32[20,128,640]{2,1,0:T(8,128)} custom-call(bf16[20,256,128]{2,1,0:T(8,128)(2,1)} %fold.6.refs_0_, bf16[20,256,128]{2,1,0:T(8,128)(2,1)} %fold.7.refs_1_, bf16[20,256,128]{2,1,0:T(8,128)(2,1)} %fold.8.refs_2_, bf16[20,256,128]{2,1,0:T(8,128)(2,1)} %fold.9.refs_3_, f32[20,1,640]{2,1,0:T(1,128)} %get-tuple-element.22.refs_4_.refs_1_, ...), custom_call_target="tpu_custom_call" | custom-call | flops 3355443200 | bytes 24903680 | tf_op jit(solution)/shard_map/analysis/pallas_call | solution.py:207
  389.8 9.2 %analysis.3 = f32[20,128,640]{2,1,0:T(8,128)} custom-call(bf16[20,256,128]{2,1,0:T(8,128)(2,1)} %fold.5.refs_0_, f32[20,1,640]{2,1,0:T(1,128)} %get-tuple-element.22.refs_4_.refs_1_, f32[20,1,640]{2,1,0:T(1,128)} %get-tuple-element.21.refs_5_.refs_2_, bf16[20,640,640]{2,1,0:T(8,128)(2,1)} %refs_3_.1, f32[20,128,640]{2,1,0:T(8,128)} %analysis.2.refs_4_), custom_call_target="tpu_custom_call" | custom-call | flops 838860800 | bytes 11141120 | tf_op jit(solution)/shard_map/analysis/pallas_call | solution.py:207
  (52 shorter events, 79.1 us)
Async XLA Ops:
  8.9 7.3 %copy-start.11 = (f32[2]{0:T(128)S(1)}, f32[2]{0:T(128)}, u32[]{:S(2)}) copy-start(f32[2]{0:T(128)} %constant.51.clone) | copy-start | bytes 28
  8.9 7.6 %copy-start.10 = (s32[640]{0:T(1024)S(1)}, s32[640]{0:T(1024)}, u32[]{:S(2)}) copy-start(s32[640]{0:T(1024)} %param.6) | copy-start | bytes 7684
  8.9 38.7 %all-to-all-start.2 = ((bf16[32,40,512]{2,1,0:T(8,128)(2,1)}), bf16[32,40,512]{2,1,0:T(8,128)(2,1)S(1)}, u32[]{:S(2)}, u32[]{:S(2)}) async-start(bf16[32,40,512]{2,1,0:T(8,128)(2,1)} %bitcast.27), calls=%async_computation.2 | async-start | bytes 2621440 | tf_op jit(solution)/shard_map/all_to_all | solution.py:276
  47.6 1.1 copy-start.5
  48.7 36.3 %all-to-all-start.8 = ((bf16[32,40,512]{2,1,0:T(8,128)(2,1)}), bf16[32,40,512]{2,1,0:T(8,128)(2,1)S(1)}, u32[]{:S(2)}, u32[]{:S(2)}) async-start(bf16[32,40,512]{2,1,0:T(8,128)(2,1)} %bitcast.30), calls=%async_computation.8 | async-start | bytes 2621440 | tf_op jit(solution)/shard_map/all_to_all | solution.py:276
  85.1 1.1 copy-start.9
  86.2 35.0 %all-to-all-start.6 = ((bf16[32,40,512]{2,1,0:T(8,128)(2,1)}), bf16[32,40,512]{2,1,0:T(8,128)(2,1)S(1)}, u32[]{:S(2)}, u32[]{:S(2)}) async-start(bf16[32,40,512]{2,1,0:T(8,128)(2,1)} %bitcast.31), calls=%async_computation.6 | async-start | bytes 2621440 | tf_op jit(solution)/shard_map/all_to_all | solution.py:276
  121.2 1.1 copy-start.8
  122.3 35.0 %all-to-all-start.4 = ((bf16[32,40,512]{2,1,0:T(8,128)(2,1)}), bf16[32,40,512]{2,1,0:T(8,128)(2,1)S(1)}, u32[]{:S(2)}, u32[]{:S(2)}) async-start(bf16[32,40,512]{2,1,0:T(8,128)(2,1)} %bitcast.29), calls=%async_computation.4 | async-start | bytes 2621440 | tf_op jit(solution)/shard_map/all_to_all | solution.py:276
  157.3 1.0 copy-start.7
  158.4 35.0 %all-to-all-start = ((bf16[32,40,512]{2,1,0:T(8,128)(2,1)}), bf16[32,40,512]{2,1,0:T(8,128)(2,1)S(1)}, u32[]{:S(2)}, u32[]{:S(2)}) async-start(bf16[32,40,512]{2,1,0:T(8,128)(2,1)} %bitcast.28), calls=%async_computation | async-start | bytes 2621440 | tf_op jit(solution)/shard_map/all_to_all | solution.py:276
  193.4 1.1 copy-start.6
  194.6 35.0 %all-to-all-start.3 = ((bf16[32,40,512]{2,1,0:T(8,128)(2,1)}), bf16[32,40,512]{2,1,0:T(8,128)(2,1)S(1)}, u32[]{:S(2)}, u32[]{:S(2)}) async-start(bf16[32,40,512]{2,1,0:T(8,128)(2,1)} %bitcast.44), calls=%async_computation.3 | async-start | bytes 2621440 | tf_op jit(solution)/shard_map/all_to_all | solution.py:276
  229.6 1.1 copy-start
  230.7 35.0 %all-to-all-start.9 = ((bf16[32,40,512]{2,1,0:T(8,128)(2,1)}), bf16[32,40,512]{2,1,0:T(8,128)(2,1)S(1)}, u32[]{:S(2)}, u32[]{:S(2)}) async-start(bf16[32,40,512]{2,1,0:T(8,128)(2,1)} %bitcast.45), calls=%async_computation.9 | async-start | bytes 2621440 | tf_op jit(solution)/shard_map/all_to_all | solution.py:276
  265.8 1.1 copy-start.1
  266.9 35.0 %all-to-all-start.7 = ((bf16[32,40,512]{2,1,0:T(8,128)(2,1)}), bf16[32,40,512]{2,1,0:T(8,128)(2,1)S(1)}, u32[]{:S(2)}, u32[]{:S(2)}) async-start(bf16[32,40,512]{2,1,0:T(8,128)(2,1)} %bitcast.46), calls=%async_computation.7 | async-start | bytes 2621440 | tf_op jit(solution)/shard_map/all_to_all | solution.py:276
  301.9 1.1 copy-start.2
  303.0 35.0 %all-to-all-start.5 = ((bf16[32,40,512]{2,1,0:T(8,128)(2,1)}), bf16[32,40,512]{2,1,0:T(8,128)(2,1)S(1)}, u32[]{:S(2)}, u32[]{:S(2)}) async-start(bf16[32,40,512]{2,1,0:T(8,128)(2,1)} %bitcast.43), calls=%async_computation.5 | async-start | bytes 2621440 | tf_op jit(solution)/shard_map/all_to_all | solution.py:276
  338.1 1.1 copy-start.3
  339.1 35.0 %all-to-all-start.1 = ((bf16[32,40,512]{2,1,0:T(8,128)(2,1)}), bf16[32,40,512]{2,1,0:T(8,128)(2,1)S(1)}, u32[]{:S(2)}, u32[]{:S(2)}) async-start(bf16[32,40,512]{2,1,0:T(8,128)(2,1)} %bitcast.42), calls=%async_computation.1 | async-start | bytes 2621440 | tf_op jit(solution)/shard_map/all_to_all | solution.py:276
  374.2 1.1 copy-start.4
